TPU v7x, 32 devices: a whole 2x2x4 slice. The times are simulated.
32 devices in a mesh: expert: 16 (over z, y, x), rep: 2 (over core).
Axes of the slice: x: 2, y: 2, z: 4, core: 2. Of those that a mesh axis runs over, the one named last changes fastest.
Arguments:
- inputs: bfloat16 [4096, 2048], P(('expert', 'rep')), may hold values from -6 to 6
- out_grad: bfloat16 [4096, 2048], P(('expert', 'rep')), may hold values from -3 to 3
- expert_ids: int32 [4096, 2], P(('expert', 'rep')), may hold values from 0 to 15, all different within a row; in each aligned block of 128 rows (0 to 127, 128 to 255, ...) at most 32 rows name the same one
- gates: float32 [4096, 2], P(('expert', 'rep')), may hold values from 0.1 to 1
- gate_w: bfloat16 [16, 2048, 768], P('expert', 'rep'), may hold values from -0.125 to 0.125
- up_w: bfloat16 [16, 2048, 768], P('expert', 'rep'), may hold values from -0.125 to 0.125
- down_w: bfloat16 [16, 768, 2048], P('expert', None, 'rep'), may hold values from -0.21875 to 0.21875
Outputs:
- input_grad: bfloat16 [4096, 2048], P(('expert', 'rep'))
- gate_w_grad: bfloat16 [16, 2048, 768], P('expert', 'rep')
- up_w_grad: bfloat16 [16, 2048, 768], P('expert', 'rep')
- down_w_grad: bfloat16 [16, 768, 2048], P('expert', None, 'rep')
Inputs may be any that keep to these rules, and one draw needn't show every extreme that they name: `expert_ids`: each row names 2 different experts; within the 128 rows of one device no expert is named more than 32 times.
All inputs are finite; a program needn't handle non-finite values.
Results may differ from a plain program's by a relative error of at most 0.0065.
Values may be sent and summed in bfloat16 or wider, within the bound.
A program may use at most 128 MiB of HBM per device.

v0:
```python
import jax
import jax.numpy as jnp
from jax import lax
from jax.sharding import PartitionSpec as P


def arrange(received, owners, local_exp, capacity):
    feature_n = received.shape[1]
    shaped = received.reshape(owners, local_exp, capacity, feature_n)
    return shaped.transpose(1, 0, 2, 3).reshape(local_exp, owners * capacity, feature_n)


def restore(slot_rows, owners, capacity):
    local_exp = slot_rows.shape[0]
    feature_n = slot_rows.shape[2]
    shaped = slot_rows.reshape(local_exp, owners, capacity, feature_n)
    return shaped.transpose(1, 0, 2, 3).reshape(owners * local_exp * capacity, feature_n)


def local(inputs, out_grad, expert_ids, gates, gate_w, up_w, down_w):
    tok_dev = inputs.shape[0]
    feature_n = inputs.shape[1]
    topk_n = expert_ids.shape[1]
    local_exp = gate_w.shape[0]
    owners = lax.axis_size("expert")
    expert_total = local_exp * owners
    capacity = 2 * tok_dev * topk_n // expert_total
    pair_count = tok_dev * topk_n
    slot_total = expert_total * capacity
    flat_ids = expert_ids.reshape(pair_count)
    one_hot = (flat_ids[:, None] == jnp.arange(expert_total, dtype=jnp.int32)[None, :]).astype(
        jnp.int32
    )
    rank_index = (
        jnp.sum(jnp.cumsum(one_hot, axis=0, dtype=jnp.int32) * one_hot, axis=1, dtype=jnp.int32) - 1
    )
    slot_index = flat_ids * capacity + rank_index
    input_pairs = jnp.repeat(inputs, topk_n, axis=0)
    scaled_pairs = (
        gates.reshape(pair_count, 1) * jnp.repeat(out_grad, topk_n, axis=0).astype(jnp.float32)
    ).astype(jnp.bfloat16)
    send_inputs = jnp.zeros((slot_total, feature_n), jnp.bfloat16).at[slot_index].set(input_pairs)
    send_grads = jnp.zeros((slot_total, feature_n), jnp.bfloat16).at[slot_index].set(scaled_pairs)
    full_gate, full_up, full_down = (
        lax.all_gather(gate_w, "rep", axis=1, tiled=True),
        lax.all_gather(up_w, "rep", axis=1, tiled=True),
        lax.all_gather(down_w, "rep", axis=2, tiled=True),
    )
    recv_inputs, recv_grads = (
        lax.all_to_all(send_inputs, "expert", split_axis=0, concat_axis=0, tiled=True),
        lax.all_to_all(send_grads, "expert", split_axis=0, concat_axis=0, tiled=True),
    )
    rows_in = arrange(recv_inputs, owners, local_exp, capacity)
    scaled_rows = arrange(recv_grads, owners, local_exp, capacity)
    gate_act = jnp.einsum("erd,edh->erh", rows_in, full_gate, preferred_element_type=jnp.float32)
    up_act = jnp.einsum("erd,edh->erh", rows_in, full_up, preferred_element_type=jnp.float32)
    gate_act, up_act = (gate_act, up_act)
    sigma = jax.nn.sigmoid(gate_act)
    silu_val = gate_act * sigma
    hidden = (silu_val * up_act).astype(jnp.bfloat16)
    hidden_grad = jnp.einsum(
        "erd,ehd->erh", scaled_rows, full_down, preferred_element_type=jnp.float32
    )
    gate_grad = (hidden_grad * up_act * sigma * (1.0 + gate_act * (1.0 - sigma))).astype(
        jnp.bfloat16
    )
    up_grad = (hidden_grad * silu_val).astype(jnp.bfloat16)
    first = jnp.einsum("erh,edh->erd", gate_grad, full_gate, preferred_element_type=jnp.float32)
    slot_grad = (
        first + jnp.einsum("erh,edh->erd", up_grad, full_up, preferred_element_type=jnp.float32)
    ).astype(jnp.bfloat16)
    returned = lax.all_to_all(
        restore(slot_grad, owners, capacity), "expert", split_axis=0, concat_axis=0, tiled=True
    )
    gate_part = jnp.einsum("erd,erh->edh", rows_in, gate_grad, preferred_element_type=jnp.float32)
    up_part = jnp.einsum("erd,erh->edh", rows_in, up_grad, preferred_element_type=jnp.float32)
    down_part = jnp.einsum("erh,erd->ehd", hidden, scaled_rows, preferred_element_type=jnp.float32)
    gate_sum, up_sum, down_sum = (
        lax.psum_scatter(
            gate_part.astype(jnp.bfloat16), "rep", scatter_dimension=1, tiled=True
        ).astype(jnp.float32),
        lax.psum_scatter(
            up_part.astype(jnp.bfloat16), "rep", scatter_dimension=1, tiled=True
        ).astype(jnp.float32),
        lax.psum_scatter(
            down_part.astype(jnp.bfloat16), "rep", scatter_dimension=2, tiled=True
        ).astype(jnp.float32),
    )
    picked = returned[slot_index]
    input_grad = jnp.sum(
        picked.reshape(tok_dev, topk_n, feature_n).astype(jnp.float32), axis=1
    ).astype(jnp.bfloat16)
    return (
        input_grad,
        gate_sum.astype(jnp.bfloat16),
        up_sum.astype(jnp.bfloat16),
        down_sum.astype(jnp.bfloat16),
    )


def solution(mesh):
    return jax.shard_map(
        local,
        mesh=mesh,
        in_specs=(
            P(("expert", "rep"), None),
            P(("expert", "rep"), None),
            P(("expert", "rep"), None),
            P(("expert", "rep"), None),
            P("expert", "rep", None),
            P("expert", "rep", None),
            P("expert", None, "rep"),
        ),
        out_specs=(
            P(("expert", "rep"), None),
            P("expert", "rep", None),
            P("expert", "rep", None),
            P("expert", None, "rep"),
        ),
        check_vma=False,
    )
```

profile of v0, /device:TPU:0, one launch (start us, length us, event | category | flops | bytes accessed | tf_op | source)
XLA Modules:
  0.0 215.6 jit_solution(12786748836473518106)
XLA Ops:
  7.2 0.0 copy-start
  7.2 0.0 all-gather.8.cloned.1.call-start
  7.2 0.7 all-gather.8.cloned.1.call-update
  7.9 0.7 broadcast_multiply_fusion
  8.6 0.8 copy.12
  9.4 0.1 eq.29
  9.5 0.1 eq.25
  9.7 0.1 copy.11
  9.8 0.1 mul.59
  9.9 0.6 reduce-window.6
  10.5 0.2 slice_reduce_fusion
  10.7 0.0 copy-done
  10.7 0.6 broadcast_in_dim.5
  11.4 0.4 reshape.167
  11.8 0.1 fusion.23
  11.9 3.7 %scatter_custom_fusion.1 = bf16[512,2048]{1,0:T(8,128)(2,1)} fusion(s32[256]{0:T(256)S(1)} %bitcast.62, bf16[256,2048]{1,0:T(8,128)(2,1)S(1)} %reshape.167, bf16[]{:T(256)} %constant.6.clone.1), kind=kCustom, calls=%fused_computation.28 | custom fusion | bytes 2097154 | tf_op jit(solution)/shard_map/scatter | solution.py:42
  15.7 0.0 copy-start.2
  15.7 0.0 copy-start.1
  15.7 8.5 %all-to-all-start.1 = ((bf16[16,32,2048]{2,1,0:T(8,128)(2,1)}), bf16[16,32,2048]{2,1,0:T(8,128)(2,1)}, u32[]{:S(2)}, u32[]{:S(2)}) async-start(bf16[16,32,2048]{2,1,0:T(8,128)(2,1)} %bitcast.6), calls=%async_computation.1 | async-start | bytes 4194304 | tf_op jit(solution)/shard_map/all_to_all | solution.py:50
  24.2 0.0 all-gather.6.cloned.1.call-start
  24.2 0.7 all-gather.6.cloned.1.call-update
  25.0 0.0 copy-done.2
  25.0 0.1 copy.15
  25.1 0.1 mul.61
  25.2 0.0 copy-done.1
  25.2 2.4 %broadcast_in_dim.4 = f32[128,2,2048]{2,1,0:T(2,128)} broadcast(bf16[128,2048]{1,0:T(8,128)(2,1)S(1)} %copy-done.1), dimensions={0,2} | broadcast | bytes 2621440 | tf_op jit(solution)/shard_map/broadcast_in_dim | solution.py:40
  27.6 2.7 %convert_element_type.59 = f32[256,2048]{1,0:T(8,128)S(1)} reshape(f32[128,2,2048]{2,1,0:T(2,128)} %broadcast_in_dim.4) | data formatting | bytes 4194304 | tf_op jit(solution)/shard_map/convert_element_type | solution.py:40
  30.3 3.8 %scatter_custom_fusion = bf16[512,2048]{1,0:T(8,128)(2,1)} fusion(s32[256]{0:T(256)S(1)} %bitcast.63, f32[256,2048]{1,0:T(8,128)S(1)} %convert_element_type.59, f32[256]{0:T(256)S(1)} %mul.61, bf16[]{:T(256)} %constant.6.clone.1), kind=kCustom, calls=%fused_computation.26 | custom fusion | flops 1048576 | bytes 4195330 | tf_op jit(solution)/shard_map/scatter | solution.py:43
  34.1 33.2 %all-to-all-done.1 = bf16[16,32,2048]{2,1,0:T(8,128)(2,1)} async-done(((bf16[16,32,2048]{2,1,0:T(8,128)(2,1)}), bf16[16,32,2048]{2,1,0:T(8,128)(2,1)}, u32[]{:S(2)}, u32[]{:S(2)}) %all-to-all-start.1) | async-done | bytes 2097184 | tf_op jit(solution)/shard_map/all_to_all | solution.py:50
  67.3 10.0 %all-to-all-start = ((bf16[16,32,2048]{2,1,0:T(8,128)(2,1)}), bf16[16,32,2048]{2,1,0:T(8,128)(2,1)S(1)}, u32[]{:S(2)}, u32[]{:S(2)}) async-start(bf16[16,32,2048]{2,1,0:T(8,128)(2,1)} %bitcast.3), calls=%async_computation | async-start | bytes 4194304 | tf_op jit(solution)/shard_map/all_to_all | solution.py:51
  77.3 0.0 all-gather.4.cloned.1.call-start
  77.3 0.7 all-gather.4.cloned.1.call-update
  78.0 0.2 reduce-scatter.8.cloned.1.call-start
  78.3 0.0 all-gather.8.cloned.1.call-done
  78.3 5.5 %fusion.2 = f32[512,768]{1,0:T(8,128)} fusion(bf16[512,2048]{1,0:T(8,128)(2,1)} %bitcast.7, bf16[1,2048,768]{2,1,0:T(8,128)(2,1)} %all-gather.8.cloned.1.call-done), kind=kOutput, calls=%fused_computation.9 | convolution fusion | flops 1610612736 | bytes 6815744 | tf_op jit(solution)/shard_map/erd,edh->erh/dot_general | solution.py:55
  83.7 0.0 all-gather.6.cloned.1.call-done
  83.7 5.5 %fusion.6 = f32[512,768]{1,0:T(8,128)} fusion(bf16[512,2048]{1,0:T(8,128)(2,1)} %bitcast.7, bf16[1,2048,768]{2,1,0:T(8,128)(2,1)} %all-gather.6.cloned.1.call-done), kind=kOutput, calls=%fused_computation.13 | convolution fusion | flops 1610612736 | bytes 6815744 | tf_op jit(solution)/shard_map/erd,edh->erh/dot_general | solution.py:56
  89.2 30.6 %all-to-all-done = bf16[16,32,2048]{2,1,0:T(8,128)(2,1)S(1)} async-done(((bf16[16,32,2048]{2,1,0:T(8,128)(2,1)}), bf16[16,32,2048]{2,1,0:T(8,128)(2,1)S(1)}, u32[]{:S(2)}, u32[]{:S(2)}) %all-to-all-start) | async-done | bytes 2097184 | tf_op jit(solution)/shard_map/all_to_all | solution.py:51
  119.8 5.5 %fusion.12 = bf16[1,768,2048]{2,1,0:T(8,128)(2,1)} fusion(bf16[512,2048]{1,0:T(8,128)(2,1)S(1)} %bitcast.59, f32[512,768]{1,0:T(8,128)} %fusion.6, f32[512,768]{1,0:T(8,128)} %fusion.2), kind=kOutput, calls=%fused_computation.19 | convolution fusion | flops 1614544896 | bytes 8388608 | tf_op jit(solution)/shard_map/erh,erd->ehd/dot_general | solution.py:77
  125.3 0.0 reduce-scatter.8.cloned.1.call-update
  125.3 0.0 reduce-scatter.6.cloned.1.call-start
  125.4 0.0 all-gather.4.cloned.1.call-done
  125.4 5.1 %multiply_convert_fusion.2 = (bf16[512,768]{1,0:T(8,128)(2,1)S(1)}, bf16[512,768]{1,0:T(8,128)(2,1)S(1)}) fusion(f32[512,768]{1,0:T(8,128)} %fusion.2, f32[512,768]{1,0:T(8,128)} %fusion.6, bf16[512,2048]{1,0:T(8,128)(2,1)S(1)} %bitcast.60, bf16[1,768,2048]{2,1,0:T(8,128)(2,1)} %all-gather.4.cloned.1.call-done), kind=kOutput, calls=%fused_computation.22 | convolution fusion | flops 1615724544 | bytes 9961472 | tf_op jit(solution)/shard_map/erd,ehd->erh/dot_general | solution.py:61
  130.5 0.0 copy-start.5
  130.5 0.0 copy-start.7
  130.5 0.9 copy-done.5
  131.4 5.3 %fusion.11 = bf16[1,2048,768]{2,1,0:T(8,128)(2,1)} fusion(bf16[512,2048]{1,0:T(8,128)(2,1)} %bitcast.7, bf16[512,768]{1,0:T(8,128)(2,1)S(1)} %get-tuple-element.4), kind=kOutput, calls=%fused_computation.18 | convolution fusion | flops 1612185600 | bytes 6029312 | tf_op jit(solution)/shard_map/erd,erh->edh/dot_general | solution.py:76
  136.7 0.0 reduce-scatter.6.cloned.1.call-update
  136.7 0.3 reduce-scatter.4.cloned.1.call-start
  137.0 0.0 copy-done.7
  137.0 5.2 %fusion.10 = bf16[1,2048,768]{2,1,0:T(8,128)(2,1)} fusion(bf16[512,2048]{1,0:T(8,128)(2,1)} %bitcast.7, bf16[512,768]{1,0:T(8,128)(2,1)S(1)} %get-tuple-element.5), kind=kOutput, calls=%fused_computation.17 | convolution fusion | flops 1612185600 | bytes 6029312 | tf_op jit(solution)/shard_map/erd,erh->edh/dot_general | solution.py:75
  142.2 0.0 copy-start.3
  142.2 0.0 reduce-scatter.4.cloned.1.call-update
  142.2 1.9 copy-done.3
  144.0 0.0 copy-start.4
  144.1 3.1 %fusion = f32[512,2048]{1,0:T(8,128)S(1)} fusion(bf16[512,768]{1,0:T(8,128)(2,1)} %copy-done.7, bf16[1,2048,768]{2,1,0:T(8,128)(2,1)S(1)} %copy-done.3), kind=kOutput, calls=%fused_computation.7 | convolution fusion | flops 1610612736 | bytes 8126464 | tf_op jit(solution)/shard_map/erh,edh->erd/dot_general | solution.py:68
  147.2 0.0 copy-done.4
  147.2 0.0 copy-done.6
  147.2 3.2 %add_convert_fusion = bf16[512,2048]{1,0:T(8,128)(2,1)} fusion(f32[512,2048]{1,0:T(8,128)S(1)} %fusion, bf16[512,768]{1,0:T(8,128)(2,1)S(1)} %copy-done.6, bf16[1,2048,768]{2,1,0:T(8,128)(2,1)S(1)} %copy-done.4), kind=kOutput, calls=%fused_computation.3 | convolution fusion | flops 1612709888 | bytes 10223616 | tf_op jit(solution)/shard_map/erh,edh->erd/dot_general | solution.py:70
  150.4 9.8 %all-to-all-start.2 = ((bf16[16,32,2048]{2,1,0:T(8,128)(2,1)}), bf16[16,32,2048]{2,1,0:T(8,128)(2,1)S(1)}, u32[]{:S(2)}, u32[]{:S(2)}) async-start(bf16[16,32,2048]{2,1,0:T(8,128)(2,1)} %bitcast.61), calls=%async_computation.2 | async-start | bytes 4194304 | tf_op jit(solution)/shard_map/all_to_all | solution.py:72
  160.1 42.9 %all-to-all-done.2 = bf16[16,32,2048]{2,1,0:T(8,128)(2,1)S(1)} async-done(((bf16[16,32,2048]{2,1,0:T(8,128)(2,1)}), bf16[16,32,2048]{2,1,0:T(8,128)(2,1)S(1)}, u32[]{:S(2)}, u32[]{:S(2)}) %all-to-all-start.2) | async-done | bytes 2097184 | tf_op jit(solution)/shard_map/all_to_all | solution.py:72
  203.0 1.4 gather_fusion
  204.4 0.7 reshape.146
  205.1 3.7 %reduce_sum.22 = bf16[128,2048]{1,0:T(8,128)(2,1)} reduce(bf16[128,2,2048]{2,1,0:T(2,128)(2,1)S(1)} %reshape.146, bf16[]{:T(256)} %constant.6.clone.1), dimensions={1}, to_apply=%region_5.6 | reduce | flops 262144 | bytes 1572866 | tf_op jit(solution)/shard_map/reduce_sum | solution.py:90
  (10 shorter events, 0.1 us)
Async XLA Ops:
  7.2 3.6 %copy-start = (bf16[128,2048]{1,0:T(8,128)(2,1)S(1)}, bf16[128,2048]{1,0:T(8,128)(2,1)}, u32[]{:S(2)}) copy-start(bf16[128,2048]{1,0:T(8,128)(2,1)} %param.7) | copy-start | bytes 1572868
  7.2 71.1 %all-gather.8.cloned.1.call-start = ((), (), s32[]{:S(2)}) async-start(), calls=%async_computation.8 | async-start | bytes 4718592 | tf_op jit(solution)/shard_map/all_gather | solution.py:45
  15.7 9.3 %copy-start.2 = (f32[128,2]{0,1:T(2,128)S(1)}, f32[128,2]{0,1:T(2,128)}, u32[]{:S(2)}) copy-start(f32[128,2]{0,1:T(2,128)} %param.10) | copy-start | bytes 3076
  15.7 9.5 %copy-start.1 = (bf16[128,2048]{1,0:T(8,128)(2,1)S(1)}, bf16[128,2048]{1,0:T(8,128)(2,1)}, u32[]{:S(2)}) copy-start(bf16[128,2048]{1,0:T(8,128)(2,1)} %param.8) | copy-start | bytes 1572868
  15.7 51.6 %all-to-all-start.1 = ((bf16[16,32,2048]{2,1,0:T(8,128)(2,1)}), bf16[16,32,2048]{2,1,0:T(8,128)(2,1)}, u32[]{:S(2)}, u32[]{:S(2)}) async-start(bf16[16,32,2048]{2,1,0:T(8,128)(2,1)} %bitcast.6), calls=%async_computation.1 | async-start | bytes 4194304 | tf_op jit(solution)/shard_map/all_to_all | solution.py:50
  24.2 59.5 %all-gather.6.cloned.1.call-start = ((), (), s32[]{:S(2)}) async-start(), calls=%async_computation.7 | async-start | bytes 4718592 | tf_op jit(solution)/shard_map/all_gather | solution.py:46
  67.3 52.5 %all-to-all-start = ((bf16[16,32,2048]{2,1,0:T(8,128)(2,1)}), bf16[16,32,2048]{2,1,0:T(8,128)(2,1)S(1)}, u32[]{:S(2)}, u32[]{:S(2)}) async-start(bf16[16,32,2048]{2,1,0:T(8,128)(2,1)} %bitcast.3), calls=%async_computation | async-start | bytes 4194304 | tf_op jit(solution)/shard_map/all_to_all | solution.py:51
  77.3 48.1 %all-gather.4.cloned.1.call-start = ((), (), s32[]{:S(2)}) async-start(), calls=%async_computation.6 | async-start | bytes 4718592 | tf_op jit(solution)/shard_map/all_gather | solution.py:47
  78.0 130.8 %reduce-scatter.8.cloned.1.call-start = ((), (), s32[]{:S(2)}) async-start(), calls=%async_computation.11 | async-start | bytes 4718592 | tf_op jit(solution)/shard_map/reduce_scatter | solution.py:85
  125.3 83.5 %reduce-scatter.6.cloned.1.call-start = ((), (), s32[]{:S(2)}) async-start(), calls=%async_computation.10 | async-start | bytes 4718592 | tf_op jit(solution)/shard_map/reduce_scatter | solution.py:82
  130.5 0.9 copy-start.5
  130.5 6.5 %copy-start.7 = (bf16[512,768]{1,0:T(8,128)(2,1)}, bf16[512,768]{1,0:T(8,128)(2,1)S(1)}, u32[]{:S(2)}) copy-start(bf16[512,768]{1,0:T(8,128)(2,1)S(1)} %get-tuple-element.5) | copy-start | bytes 2359300
  136.7 72.1 %reduce-scatter.4.cloned.1.call-start = ((), (), s32[]{:S(2)}) async-start(), calls=%async_computation.9 | async-start | bytes 4718592 | tf_op jit(solution)/shard_map/reduce_scatter | solution.py:79
  142.2 1.9 copy-start.3
  144.0 3.1 %copy-start.4 = (bf16[1,2048,768]{2,1,0:T(8,128)(2,1)S(1)}, bf16[1,2048,768]{2,1,0:T(8,128)(2,1)}, u32[]{:S(2)}) copy-start(bf16[1,2048,768]{2,1,0:T(8,128)(2,1)} %all-gather.6.cloned.1.call-done) | copy-start | bytes 9437188
  144.0 3.1 %copy-start.6 = (bf16[512,768]{1,0:T(8,128)(2,1)S(1)}, bf16[512,768]{1,0:T(8,128)(2,1)}, u32[]{:S(2)}) copy-start(bf16[512,768]{1,0:T(8,128)(2,1)} %copy-done.5) | copy-start | bytes 2359300
  150.4 52.6 %all-to-all-start.2 = ((bf16[16,32,2048]{2,1,0:T(8,128)(2,1)}), bf16[16,32,2048]{2,1,0:T(8,128)(2,1)S(1)}, u32[]{:S(2)}, u32[]{:S(2)}) async-start(bf16[16,32,2048]{2,1,0:T(8,128)(2,1)} %bitcast.61), calls=%async_computation.2 | async-start | bytes 4194304 | tf_op jit(solution)/shard_map/all_to_all | solution.py:72
Sparse Core Ops, SparseCore 0:
  9.6 14.8 all-gather.7
  26.6 13.3 all-gather.5
  79.7 13.4 all-gather.3
  125.4 15.0 reduce-scatter.7
  143.3 12.0 reduce-scatter.5
  158.0 12.0 reduce-scatter.3
where the time goes:
time: 220 us; the launch traced here: 216 us
  waiting for transfers between devices  109 us (50%)
  matrix products  38.2 us (17%)
  starting transfers between devices  28.9 us (13%)
  local copies, waits for them, and re-layouts  16.5 us (8%)
  between operations  14.3 us (6%)
  other arithmetic  8.94 us (4%)
    all_to_all x1, waiting for transfers between devices, local(): lax.all_to_all(restore(slot_grad, owners, capacity), 'expert', split_axis...  42.9 us
    all_to_all x1, waiting for transfers between devices, local(): lax.all_to_all(send_inputs, 'expert', split_axis=0, concat_axis=0, tiled=...  33.2 us
    all_to_all x1, waiting for transfers between devices, local(): lax.all_to_all(send_grads, 'expert', split_axis=0, concat_axis=0, tiled=T...  30.6 us
    all_to_all x1, starting transfers between devices, local(): lax.all_to_all(send_grads, 'expert', split_axis=0, concat_axis=0, tiled=T...  9.97 us
    all_to_all x1, starting transfers between devices, local(): lax.all_to_all(restore(slot_grad, owners, capacity), 'expert', split_axis...  9.76 us
    all_to_all x1, starting transfers between devices, local(): lax.all_to_all(send_inputs, 'expert', split_axis=0, concat_axis=0, tiled=...  8.5 us
    dot_general x1, matrix products, local(): jnp.einsum('erh,erd->ehd', hidden, scaled_rows, preferred_element_type=jn...  5.5 us
    dot_general x1, matrix products, local(): jnp.einsum('erd,edh->erh', rows_in, full_up, preferred_element_type=jnp.f...  5.46 us
  transfers between devices with their start and end apart: 9, of which 3 were waited for; matrix products, arithmetic and copies ran while one was open for 28% of the time, Pallas kernels for 0%

commit v1 on v0

--- a/solution.py
+++ b/solution.py
@@ -1,7 +1,430 @@
+import functools
+
 import jax
 import jax.numpy as jnp
 from jax import lax
+from jax.experimental import pallas as pl
+from jax.experimental.pallas import tpu as pltpu
 from jax.sharding import PartitionSpec as P
+
+MESH = pl.DeviceIdType.MESH
+COLS = 4
+F32 = jnp.float32
+BF16 = jnp.bfloat16
+NT = (((1,), (1,)), ((), ()))
+TN = (((0,), (0,)), ((), ()))
+
+
+def layer_kernel(
+    planes, experts, cap,
+    ids_ref, gates_ref, x_hbm, g_hbm, gw_hbm, uw_hbm, dw_hbm,
+    out_ref, gwo_ref, uwo_ref, dwo_ref,
+    xg, gg, meta, st_x, st_g, rows, scaled, sel_t, wg, wu, wd, ga, ua,
+    hid, gate_gr, up_gr, rows_h, scaled_h, sg, ret, rcv, snd,
+    load_sem, w_send, w_recv, zm_s, zm_r, zx_s, zx_r, zg_s, zg_r,
+    px_s, px_r, pg_s, pg_r, pr_s, pr_r, zr_s, zr_r, rep_s, rep_r, loc_sem,
+):
+    e, r = lax.axis_index("expert"), lax.axis_index("rep")
+    z, c = e // COLS, e % COLS
+    other = 1 - r
+    tok = x_hbm.shape[0]
+    last = planes - 1
+    slots = COLS * cap
+    half = gw_hbm.shape[1]
+    feat = x_hbm.shape[1]
+    hidden_n = gw_hbm.shape[2]
+    total = planes * slots
+
+    def al(v, m):
+        return pl.multiple_of(v, m)
+
+    w_at = [
+        (gw_hbm.at[0], wg.at[pl.ds(al(r * half, half), half)]),
+        (uw_hbm.at[0], wu.at[pl.ds(al(r * half, half), half)]),
+        (dw_hbm.at[0], wd.at[:, pl.ds(al(r * half, half), half)]),
+    ]
+    load_x = pltpu.make_async_copy(x_hbm, xg.at[z], load_sem.at[0])
+    load_g = pltpu.make_async_copy(g_hbm, gg.at[z], load_sem.at[1])
+    load_x.start()
+    load_g.start()
+    load_w = [pltpu.make_async_copy(s, d, load_sem.at[2 + i]) for i, (s, d) in enumerate(w_at)]
+    for cp in load_w:
+        cp.start()
+
+    barrier = pltpu.get_barrier_semaphore()
+    for j in range(1, COLS):
+        pl.semaphore_signal(barrier, inc=1, device_id=(z * COLS + (c + j) % COLS, r), device_id_type=MESH)
+    pl.semaphore_signal(barrier, inc=1, device_id=(e, other), device_id_type=MESH)
+
+    @pl.when(z < last)
+    def _():
+        pl.semaphore_signal(barrier, inc=1, device_id=(e + COLS, r), device_id_type=MESH)
+
+    @pl.when(z > 0)
+    def _():
+        pl.semaphore_signal(barrier, inc=1, device_id=(e - COLS, r), device_id_type=MESH)
+
+    id0, id1 = ids_ref[0:1, :], ids_ref[1:2, :]
+    exp_iota = lax.broadcasted_iota(jnp.int32, (experts, tok), 0)
+    one0 = jnp.where(exp_iota == id0, 1.0, 0.0)
+    one1 = jnp.where(exp_iota == id1, 1.0, 0.0)
+    before = jnp.where(
+        lax.broadcasted_iota(jnp.int32, (tok, tok), 0) < lax.broadcasted_iota(jnp.int32, (tok, tok), 1), 1.0, 0.0
+    ).astype(BF16)
+    rank = jnp.dot((one0 + one1).astype(BF16), before, preferred_element_type=F32)
+    slot0 = jnp.sum(rank * one0, axis=0, keepdims=True) + id0.astype(F32) * cap
+    slot1 = jnp.sum(rank * one1, axis=0, keepdims=True) + id1.astype(F32) * cap
+    meta[z] = jnp.concatenate(
+        [slot0, slot1, gates_ref[0:1, :], gates_ref[1:2, :], jnp.zeros((4, tok), F32)], axis=0
+    )
+    neighbours = COLS + jnp.where(z < last, 1, 0) + jnp.where(z > 0, 1, 0)
+    pl.semaphore_wait(barrier, neighbours)
+
+    def up(buf, ss, rs, k):
+        return pltpu.make_async_remote_copy(
+            src_ref=buf.at[jnp.maximum(z - k, 0)], dst_ref=buf.at[jnp.maximum(z - k, 0)],
+            send_sem=ss.at[0, k], recv_sem=rs.at[0, k], device_id=(e + COLS, r), device_id_type=MESH)
+
+    def down(buf, ss, rs, k):
+        return pltpu.make_async_remote_copy(
+            src_ref=buf.at[jnp.minimum(z + k, last)], dst_ref=buf.at[jnp.minimum(z + k, last)],
+            send_sem=ss.at[1, k], recv_sem=rs.at[1, k], device_id=(e - COLS, r), device_id_type=MESH)
+
+    def can_up(k):
+        return (z < last) & (z - k >= 0)
+
+    def can_down(k):
+        return (z > 0) & (z + k <= last)
+
+    def chain_start(buf, ss, rs, k):
+        @pl.when(can_up(k))
+        def _():
+            up(buf, ss, rs, k).start()
+
+        @pl.when(can_down(k))
+        def _():
+            down(buf, ss, rs, k).start()
+
+    def chain_wait(buf, ss, rs, k):
+        @pl.when(z - 1 - k >= 0)
+        def _():
+            b = buf.at[jnp.maximum(z - 1 - k, 0)]
+            pltpu.make_async_remote_copy(
+                src_ref=b, dst_ref=b, send_sem=ss.at[0, k], recv_sem=rs.at[0, k],
+                device_id=(e, other), device_id_type=MESH).wait_recv()
+
+        @pl.when(z + 1 + k <= last)
+        def _():
+            b = buf.at[jnp.minimum(z + 1 + k, last)]
+            pltpu.make_async_remote_copy(
+                src_ref=b, dst_ref=b, send_sem=ss.at[1, k], recv_sem=rs.at[1, k],
+                device_id=(e, other), device_id_type=MESH).wait_recv()
+
+    def chain_drain(buf, ss, rs):
+        for k in range(planes - 1):
+            @pl.when(can_up(k))
+            def _(k=k):
+                up(buf, ss, rs, k).wait_send()
+
+            @pl.when(can_down(k))
+            def _(k=k):
+                down(buf, ss, rs, k).wait_send()
+
+    def plane_copy(st, dst, ss, rs, p, j):
+        d = (c + j) % COLS
+        return pltpu.make_async_remote_copy(
+            src_ref=st.at[p, pl.ds(al(d * cap, cap), cap)],
+            dst_ref=dst.at[p, pl.ds(al(c * cap, cap), cap)],
+            send_sem=ss.at[p, j - 1], recv_sem=rs.at[p, j - 1],
+            device_id=(z * COLS + d, r), device_id_type=MESH)
+
+    def plane_send(st, dst, ss, rs, p):
+        for j in range(1, COLS):
+            plane_copy(st, dst, ss, rs, p, j).start()
+        dst[p, pl.ds(al(c * cap, cap), cap), :] = st[p, pl.ds(al(c * cap, cap), cap), :]
+
+    def plane_wait(st, dst, ss, rs, p):
+        for j in range(1, COLS):
+            plane_copy(st, dst, ss, rs, p, j).wait_recv()
+
+    def plane_drain(st, dst, ss, rs):
+        for p in range(planes):
+            for j in range(1, COLS):
+                plane_copy(st, dst, ss, rs, p, j).wait_send()
+
+    def selection(p):
+        m = meta[p]
+        place = (lax.broadcasted_iota(jnp.int32, (slots, tok), 0) + z * slots).astype(F32)
+        return jnp.where(place == m[0:1, :], 1.0, 0.0), jnp.where(place == m[1:2, :], 1.0, 0.0), m
+
+    def dispatch_x(p):
+        s0, s1, _ = selection(p)
+        pick = s0 + s1
+        sel_t[p] = pick.T.astype(BF16)
+        st_x[p] = jnp.dot(pick.astype(BF16), xg[p], preferred_element_type=F32).astype(BF16)
+        plane_send(st_x, rows, px_s, px_r, p)
+
+    def dispatch_g(p):
+        s0, s1, m = selection(p)
+        gate = jnp.sum(s0 * m[2:3, :] + s1 * m[3:4, :], axis=1, keepdims=True)
+        picked = jnp.dot((s0 + s1).astype(BF16), gg[p], preferred_element_type=F32)
+        st_g[p] = (picked * gate).astype(BF16)
+        plane_send(st_g, scaled, pg_s, pg_r, p)
+
+    def both(fn, k):
+        @pl.when(z - 1 - k >= 0)
+        def _():
+            fn(jnp.maximum(z - 1 - k, 0))
+
+        @pl.when(z + 1 + k <= last)
+        def _():
+            fn(jnp.minimum(z + 1 + k, last))
+
+    chain_start(meta, zm_s, zm_r, 0)
+    load_x.wait()
+    chain_start(xg, zx_s, zx_r, 0)
+
+    def w_copy(i):
+        s, d = w_at[i]
+        return pltpu.make_async_remote_copy(
+            src_ref=s, dst_ref=d, send_sem=w_send.at[i], recv_sem=w_recv.at[i],
+            device_id=(e, other), device_id_type=MESH)
+
+    for i in range(3):
+        w_copy(i).start()
+    load_g.wait()
+    dispatch_x(z)
+    for k in range(planes - 1):
+        chain_wait(meta, zm_s, zm_r, k)
+        chain_wait(xg, zx_s, zx_r, k)
+        if k < planes - 2:
+            chain_start(meta, zm_s, zm_r, k + 1)
+            chain_start(xg, zx_s, zx_r, k + 1)
+        if k == planes - 3:
+            chain_start(gg, zg_s, zg_r, 0)
+        both(dispatch_x, k)
+    dispatch_g(z)
+    chain_wait(gg, zg_s, zg_r, 0)
+    chain_start(gg, zg_s, zg_r, 1)
+    both(dispatch_g, 0)
+    for cp in load_w:
+        cp.wait()
+    for i in range(3):
+        w_copy(i).wait()
+    for p in range(planes):
+        plane_wait(st_x, rows, px_s, px_r, p)
+
+    def halves(src, dst, i):
+        lo = pl.ds(al(r * half, half), half)
+        hi = pl.ds(al(other * half, half), half)
+        return (
+            pltpu.make_async_copy(src.at[:, :, lo], dst.at[r], loc_sem.at[i]),
+            pltpu.make_async_remote_copy(
+                src_ref=src.at[:, :, hi], dst_ref=dst.at[r], send_sem=rep_s.at[i], recv_sem=rep_r.at[i],
+                device_id=(e, other), device_id_type=MESH),
+        )
+
+    rows_cp = halves(rows, rows_h, 0)
+    for cp in rows_cp:
+        cp.start()
+    step_h = 256 if hidden_n % 256 == 0 else hidden_n
+
+    @pl.loop(0, hidden_n // step_h)
+    def _(i):
+        cols = pl.ds(al(i * step_h, step_h), step_h)
+        a = rows[...].reshape(total, feat)
+        ga[:, cols] = jnp.dot(a, wg[:, cols], preferred_element_type=F32)
+        ua[:, cols] = jnp.dot(a, wu[:, cols], preferred_element_type=F32)
+
+    for k in range(1, planes - 1):
+        chain_wait(gg, zg_s, zg_r, k)
+        if k < planes - 2:
+            chain_start(gg, zg_s, zg_r, k + 1)
+        both(dispatch_g, k)
+    for p in range(planes):
+        plane_wait(st_g, scaled, pg_s, pg_r, p)
+    scaled_cp = halves(scaled, scaled_h, 1)
+    for cp in scaled_cp:
+        cp.start()
+
+    @pl.loop(0, hidden_n // step_h)
+    def _(i):
+        cols = pl.ds(al(i * step_h, step_h), step_h)
+        hg = lax.dot_general(scaled[...].reshape(total, feat), wd[cols, :], NT, preferred_element_type=F32)
+        gate_act, up_act = ga[:, cols], ua[:, cols]
+        sigma = jax.nn.sigmoid(gate_act)
+        silu = gate_act * sigma
+        hid[r, :, cols] = (silu * up_act).astype(BF16)
+        gate_gr[r, :, cols] = (hg * up_act * sigma * (1.0 + gate_act * (1.0 - sigma))).astype(BF16)
+        up_gr[r, :, cols] = (hg * silu).astype(BF16)
+
+    def rep_copy(ref, i):
+        return pltpu.make_async_remote_copy(
+            src_ref=ref.at[r], dst_ref=ref.at[r], send_sem=rep_s.at[i], recv_sem=rep_r.at[i],
+            device_id=(e, other), device_id_type=MESH)
+
+    rep_cp = [rep_copy(ref, 2 + i) for i, ref in enumerate((gate_gr, up_gr, hid))]
+    for cp in rep_cp:
+        cp.start()
+    step_d = 256
+
+    @pl.loop(0, feat // step_d)
+    def _(i):
+        cols = pl.ds(al(i * step_d, step_d), step_d)
+        v = lax.dot_general(gate_gr[r], wg[cols, :], NT, preferred_element_type=F32)
+        v = v + lax.dot_general(up_gr[r], wu[cols, :], NT, preferred_element_type=F32)
+        sg[:, :, cols] = v.astype(BF16).reshape(planes, slots, step_d)
+
+    order = sorted(range(planes), key=lambda p: min(p, last - p))
+    for p in order:
+        plane_send(sg, ret, pr_s, pr_r, p)
+
+    def part(p):
+        return jnp.dot(sel_t[p], ret[p], preferred_element_type=F32)
+
+    def ret_copy(way, p):
+        return pltpu.make_async_remote_copy(
+            src_ref=snd.at[p], dst_ref=rcv.at[way, p], send_sem=zr_s.at[p], recv_sem=zr_r.at[way, p],
+            device_id=(e + COLS if way == 0 else e - COLS, r), device_id_type=MESH)
+
+    def ret_wait(way, p):
+        pltpu.make_async_remote_copy(
+            src_ref=snd.at[p], dst_ref=rcv.at[way, p], send_sem=zr_s.at[p], recv_sem=zr_r.at[way, p],
+            device_id=(e, other), device_id_type=MESH).wait_recv()
+
+    def forward(way, p, first):
+        @pl.when(first)
+        def _():
+            snd[p] = part(p).astype(BF16)
+
+        @pl.when(jnp.logical_not(first))
+        def _():
+            ret_wait(way, p)
+            snd[p] = (part(p) + rcv[way, p].astype(F32)).astype(BF16)
+
+        ret_copy(way, p).start()
+
+    def weight_in(a_half, grads, out):
+        step = 256
+
+        @pl.loop(0, half // step)
+        def _(i):
+            cols = pl.ds(al(i * step, step), step)
+            v = lax.dot_general(a_half[0, :, :, cols].reshape(total, step), grads[0], TN, preferred_element_type=F32)
+            v = v + lax.dot_general(a_half[1, :, :, cols].reshape(total, step), grads[1], TN, preferred_element_type=F32)
+            out[0, cols, :] = v.astype(BF16)
+
+    def weight_down():
+        @pl.loop(0, hidden_n // step_h)
+        def _(i):
+            cols = pl.ds(al(i * step_h, step_h), step_h)
+            v = lax.dot_general(hid[0, :, cols], scaled_h[0].reshape(total, half), TN, preferred_element_type=F32)
+            v = v + lax.dot_general(hid[1, :, cols], scaled_h[1].reshape(total, half), TN, preferred_element_type=F32)
+            dwo_ref[0, cols, :] = v.astype(BF16)
+
+    for p in order:
+        plane_wait(sg, ret, pr_s, pr_r, p)
+    for k in range(planes):
+        @pl.when(k < z)
+        def _(k=k):
+            forward(1, k, z == last)
+
+        @pl.when(last - k > z)
+        def _(k=k):
+            forward(0, last - k, z == 0)
+
+        if k == 0:
+            for cp in (rows_cp, scaled_cp):
+                cp[0].wait()
+                cp[1].wait()
+            for cp in rep_cp:
+                cp.wait()
+            weight_in(rows_h, gate_gr, gwo_ref)
+        elif k == 1:
+            weight_in(rows_h, up_gr, uwo_ref)
+        elif k == 2:
+            weight_down()
+
+    own = part(z)
+    snd[z] = own.astype(BF16)
+
+    @pl.when(z < last)
+    def _():
+        ret_wait(1, z)
+
+    @pl.when(z > 0)
+    def _():
+        ret_wait(0, z)
+
+    above = jnp.where(z < last, rcv[1, z].astype(F32), 0.0)
+    below = jnp.where(z > 0, rcv[0, z].astype(F32), 0.0)
+    out_ref[...] = (own + above + below).astype(BF16)
+
+    chain_drain(meta, zm_s, zm_r)
+    chain_drain(xg, zx_s, zx_r)
+    chain_drain(gg, zg_s, zg_r)
+    plane_drain(st_x, rows, px_s, px_r)
+    plane_drain(st_g, scaled, pg_s, pg_r)
+    plane_drain(sg, ret, pr_s, pr_r)
+    for p in range(planes):
+        @pl.when(p < z)
+        def _(p=p):
+            ret_copy(1, p).wait_send()
+
+        @pl.when(p > z)
+        def _(p=p):
+            ret_copy(0, p).wait_send()
+
+
+def chained(inputs, out_grad, expert_ids, gates, gate_w, up_w, down_w):
+    tok, feat = inputs.shape
+    half, hidden_n = gate_w.shape[1], gate_w.shape[2]
+    experts = lax.axis_size("expert")
+    planes = experts // COLS
+    cap = 2 * tok * expert_ids.shape[1] // experts
+    slots = COLS * cap
+    total = planes * slots
+    dma = pltpu.SemaphoreType.DMA
+    vmem = pl.BlockSpec(memory_space=pltpu.VMEM)
+    hbm = pl.BlockSpec(memory_space=pl.ANY)
+    block = (planes, slots, feat)
+    scratch = [
+        pltpu.VMEM((planes, tok, feat), BF16), pltpu.VMEM((planes, tok, feat), BF16),
+        pltpu.VMEM((planes, 8, tok), F32),
+        pltpu.VMEM(block, BF16), pltpu.VMEM(block, BF16), pltpu.VMEM(block, BF16), pltpu.VMEM(block, BF16),
+        pltpu.VMEM((planes, tok, slots), BF16),
+        pltpu.VMEM((feat, hidden_n), BF16), pltpu.VMEM((feat, hidden_n), BF16), pltpu.VMEM((hidden_n, feat), BF16),
+        pltpu.VMEM((total, hidden_n), F32), pltpu.VMEM((total, hidden_n), F32),
+        pltpu.VMEM((2, total, hidden_n), BF16), pltpu.VMEM((2, total, hidden_n), BF16),
+        pltpu.VMEM((2, total, hidden_n), BF16),
+        pltpu.VMEM((2, planes, slots, half), BF16), pltpu.VMEM((2, planes, slots, half), BF16),
+        pltpu.VMEM(block, BF16), pltpu.VMEM(block, BF16),
+        pltpu.VMEM((2, planes, tok, feat), BF16), pltpu.VMEM((planes, tok, feat), BF16),
+        dma((5,)), dma((3,)), dma((3,)),
+        dma((2, planes - 1)), dma((2, planes - 1)), dma((2, planes - 1)), dma((2, planes - 1)),
+        dma((2, planes - 1)), dma((2, planes - 1)),
+        dma((planes, COLS - 1)), dma((planes, COLS - 1)), dma((planes, COLS - 1)), dma((planes, COLS - 1)),
+        dma((planes, COLS - 1)), dma((planes, COLS - 1)),
+        dma((planes,)), dma((2, planes)), dma((5,)), dma((5,)), dma((2,)),
+    ]
+    return pl.pallas_call(
+        functools.partial(layer_kernel, planes, experts, cap),
+        out_shape=(
+            jax.ShapeDtypeStruct((tok, feat), BF16),
+            jax.ShapeDtypeStruct(gate_w.shape, BF16),
+            jax.ShapeDtypeStruct(up_w.shape, BF16),
+            jax.ShapeDtypeStruct(down_w.shape, BF16),
+        ),
+        in_specs=[vmem, vmem] + [hbm] * 5,
+        out_specs=(vmem,) * 4,
+        scratch_shapes=scratch,
+        compiler_params=pltpu.CompilerParams(
+            collective_id=0, has_side_effects=True, vmem_limit_bytes=60 * 1024 * 1024
+        ),
+        cost_estimate=pl.CostEstimate(
+            flops=18 * total * feat * hidden_n, bytes_accessed=8 * feat * hidden_n, transcendentals=total * hidden_n
+        ),
+    )(expert_ids.T, gates.T, inputs, out_grad, gate_w, up_w, down_w)
 
 
 def arrange(received, owners, local_exp, capacity):
@@ -18,6 +441,8 @@
 
 
 def local(inputs, out_grad, expert_ids, gates, gate_w, up_w, down_w):
+    if lax.axis_size("expert") <= 16:
+        return chained(inputs, out_grad, expert_ids, gates, gate_w, up_w, down_w)
     tok_dev = inputs.shape[0]
     feature_n = inputs.shape[1]
     topk_n = expert_ids.shape[1]

time: 220 us -> 167 us (0.76)
  the two profiles are of different devices: /device:TPU:0 before, /device:TPU:10 now
where the time goes in v1:
time: 167 us
  Pallas kernels  159 us (95%)
  local copies, waits for them, and re-layouts  7.77 us (5%)
    pallas_call x1, Pallas kernels, chained(): pl.pallas_call(functools.partial(layer_kernel, planes, experts, cap), out...  159 us
    unnamed x8, local copies, waits for them, and re-layouts  7.77 us

profile of v1, /device:TPU:10, one launch (start us, length us, event | category | flops | bytes accessed | tf_op | source)
XLA Modules:
  0.0 167.2 jit_solution(16228848050628029232)
XLA Ops:
  0.6 158.7 %shard_map.102 = (bf16[128,2048]{1,0:T(8,128)(2,1)}, bf16[1,1024,768]{2,1,0:T(8,128)(2,1)}, bf16[1,1024,768]{2,1,0:T(8,128)(2,1)}, bf16[1,768,1024]{2,1,0:T(8,128)(2,1)}) custom-call(s32[2,128]{1,0:T(2,128)} %bitcast.2, f32[2,128]{1,0:T(2,128)} %bitcast.3, bf16[128,2048]{1,0:T(8,128)(2,1)} %x_hbm.1, bf16[128,2048]{1,0:T(8,128)(2,1)} %g_hbm.1, ...), custom_call_target="tpu_custom_call" | custom-call | flops 14495514624 | bytes 12582912 | tf_op jit(solution)/shard_map/pallas_call | solution.py:410
  159.4 1.9 %copy.15 = bf16[128,2048]{1,0:T(8,128)(2,1)} copy(bf16[128,2048]{1,0:T(8,128)(2,1)} %get-tuple-element.8) | data formatting | bytes 1048576
  161.3 0.0 copy-start.1
  161.3 2.8 %copy.16 = bf16[1,1024,768]{2,1,0:T(8,128)(2,1)} copy(bf16[1,1024,768]{2,1,0:T(8,128)(2,1)} %get-tuple-element.9) | data formatting | bytes 3145728
  164.0 0.0 copy-done.1
  164.0 0.0 copy-start
  164.0 1.1 copy.17
  165.2 0.8 copy-done
  166.0 1.1 copy.18
Async XLA Ops:
  161.3 2.8 %copy-start.1 = (bf16[1,1024,768]{2,1,0:T(8,128)(2,1)S(1)}, bf16[1,1024,768]{2,1,0:T(8,128)(2,1)}, u32[]{:S(2)}) copy-start(bf16[1,1024,768]{2,1,0:T(8,128)(2,1)} %get-tuple-element.10) | copy-start | bytes 4718596
  164.0 2.0 %copy-start = (bf16[1,768,1024]{2,1,0:T(8,128)(2,1)S(1)}, bf16[1,768,1024]{2,1,0:T(8,128)(2,1)}, u32[]{:S(2)}) copy-start(bf16[1,768,1024]{2,1,0:T(8,128)(2,1)} %get-tuple-element.11) | copy-start | bytes 4718596

commit v2 on v1

--- a/solution.py
+++ b/solution.py
@@ -9,6 +9,7 @@
 
 MESH = pl.DeviceIdType.MESH
 COLS = 4
+PIECES = 4
 F32 = jnp.float32
 BF16 = jnp.bfloat16
 NT = (((1,), (1,)), ((), ()))
@@ -21,8 +22,9 @@
     out_ref, gwo_ref, uwo_ref, dwo_ref,
     xg, gg, meta, st_x, st_g, rows, scaled, sel_t, wg, wu, wd, ga, ua,
     hid, gate_gr, up_gr, rows_h, scaled_h, sg, ret, rcv, snd,
+    own_part, gwo_v, uwo_v, dwo_v,
     load_sem, w_send, w_recv, zm_s, zm_r, zx_s, zx_r, zg_s, zg_r,
-    px_s, px_r, pg_s, pg_r, pr_s, pr_r, zr_s, zr_r, rep_s, rep_r, loc_sem,
+    px_s, px_r, pg_s, pg_r, pr_s, pr_r, zr_s, zr_r, rep_s, rep_r, loc_sem, out_sem,
 ):
     e, r = lax.axis_index("expert"), lax.axis_index("rep")
     z, c = e // COLS, e % COLS
@@ -180,185 +182,207 @@
         def _():
             fn(jnp.minimum(z + 1 + k, last))
 
-    chain_start(meta, zm_s, zm_r, 0)
-    load_x.wait()
-    chain_start(xg, zx_s, zx_r, 0)
-
     def w_copy(i):
         s, d = w_at[i]
         return pltpu.make_async_remote_copy(
             src_ref=s, dst_ref=d, send_sem=w_send.at[i], recv_sem=w_recv.at[i],
             device_id=(e, other), device_id_type=MESH)
 
+    def halves(src, dst, i, p):
+        lo = pl.ds(al(r * half, half), half)
+        hi = pl.ds(al(other * half, half), half)
+        return (
+            pltpu.make_async_copy(src.at[p, :, lo], dst.at[r, p], loc_sem.at[i, p]),
+            pltpu.make_async_remote_copy(
+                src_ref=src.at[p, :, hi], dst_ref=dst.at[r, p], send_sem=rep_s.at[i, p], recv_sem=rep_r.at[i, p],
+                device_id=(e, other), device_id_type=MESH),
+        )
+
+    def rep_copy(ref, i, p):
+        return pltpu.make_async_remote_copy(
+            src_ref=ref.at[r, p], dst_ref=ref.at[r, p], send_sem=rep_s.at[i, p], recv_sem=rep_r.at[i, p],
+            device_id=(e, other), device_id_type=MESH)
+
+    step_h = 256 if hidden_n % 256 == 0 else hidden_n
+    step_d = 512
+
+    def acts(p):
+        plane_wait(st_x, rows, px_s, px_r, p)
+        for cp in halves(rows, rows_h, 0, p):
+            cp.start()
+
+        @pl.loop(0, hidden_n // step_h)
+        def _(i):
+            cols = pl.ds(al(i * step_h, step_h), step_h)
+            ga[p, :, cols] = jnp.dot(rows[p], wg[:, cols], preferred_element_type=F32)
+            ua[p, :, cols] = jnp.dot(rows[p], wu[:, cols], preferred_element_type=F32)
+
+    def grads(p):
+        plane_wait(st_g, scaled, pg_s, pg_r, p)
+        for cp in halves(scaled, scaled_h, 1, p):
+            cp.start()
+
+        @pl.loop(0, hidden_n // step_h)
+        def _(i):
+            cols = pl.ds(al(i * step_h, step_h), step_h)
+            hg = lax.dot_general(scaled[p], wd[cols, :], NT, preferred_element_type=F32)
+            gate_act, up_act = ga[p, :, cols], ua[p, :, cols]
+            sigma = jax.nn.sigmoid(gate_act)
+            silu = gate_act * sigma
+            hid[r, p, :, cols] = (silu * up_act).astype(BF16)
+            gate_gr[r, p, :, cols] = (hg * up_act * sigma * (1.0 + gate_act * (1.0 - sigma))).astype(BF16)
+            up_gr[r, p, :, cols] = (hg * silu).astype(BF16)
+
+        @pl.loop(0, feat // step_d)
+        def _(i):
+            cols = pl.ds(al(i * step_d, step_d), step_d)
+            v = lax.dot_general(gate_gr[r, p], wg[cols, :], NT, preferred_element_type=F32)
+            v = v + lax.dot_general(up_gr[r, p], wu[cols, :], NT, preferred_element_type=F32)
+            sg[p, :, cols] = v.astype(BF16)
+
+        plane_send(sg, ret, pr_s, pr_r, p)
+        for i, ref in enumerate((gate_gr, up_gr, hid)):
+            rep_copy(ref, 2 + i, p).start()
+
+    piece = tok // PIECES
+
+    def ret_copy(way, p, q):
+        at = pl.ds(q * piece, piece)
+        return pltpu.make_async_remote_copy(
+            src_ref=snd.at[p, at], dst_ref=rcv.at[way, p, at], send_sem=zr_s.at[p, q], recv_sem=zr_r.at[way, p, q],
+            device_id=(jnp.where(way == 0, e + COLS, e - COLS), r), device_id_type=MESH)
+
+    def ret_wait(way, p, q):
+        at = pl.ds(q * piece, piece)
+        pltpu.make_async_remote_copy(
+            src_ref=snd.at[p, at], dst_ref=rcv.at[way, p, at], send_sem=zr_s.at[p, q], recv_sem=zr_r.at[way, p, q],
+            device_id=(e, other), device_id_type=MESH).wait_recv()
+
+    def forward(way, p, first):
+        plane_wait(sg, ret, pr_s, pr_r, p)
+        own_part[...] = jnp.dot(sel_t[p], ret[p], preferred_element_type=F32)
+        for q in range(PIECES):
+            at = pl.ds(q * piece, piece)
+
+            @pl.when(first)
+            def _():
+                snd[p, at, :] = own_part[at, :].astype(BF16)
+
+            @pl.when(jnp.logical_not(first))
+            def _():
+                ret_wait(way, p, q)
+                snd[p, at, :] = (own_part[at, :] + rcv[way, p, at, :].astype(F32)).astype(BF16)
+
+            ret_copy(way, p, q).start()
+
+    def forward_both(k):
+        @pl.loop(0, 2)
+        def _(side):
+            way = jnp.where(z >= planes // 2, 1 - side, side)
+            p = jnp.where(way == 1, last - 1 - k, k + 1)
+
+            @pl.when(((way == 1) & (p < z)) | ((way == 0) & (p > z)))
+            def _():
+                forward(way, p, ((way == 1) & (z == last)) | ((way == 0) & (z == 0)))
+
+    def weight_in(a_half, grad, out):
+        step = 256
+
+        @pl.loop(0, half // step)
+        def _(i):
+            cols = pl.ds(al(i * step, step), step)
+            v = 0.0
+            for rep in range(2):
+                v = v + lax.dot_general(
+                    a_half[rep, :, :, cols].reshape(total, step), grad[rep].reshape(total, hidden_n), TN,
+                    preferred_element_type=F32)
+            out[0, cols, :] = v.astype(BF16)
+
+    def weight_down():
+        @pl.loop(0, hidden_n // step_h)
+        def _(i):
+            cols = pl.ds(al(i * step_h, step_h), step_h)
+            v = 0.0
+            for rep in range(2):
+                v = v + lax.dot_general(
+                    hid[rep, :, :, cols].reshape(total, step_h), scaled_h[rep].reshape(total, half), TN,
+                    preferred_element_type=F32)
+            dwo_v[0, cols, :] = v.astype(BF16)
+
+    def out_copy(i):
+        src, dst = ((gwo_v, gwo_ref), (uwo_v, uwo_ref), (dwo_v, dwo_ref))[i]
+        return pltpu.make_async_copy(src, dst, out_sem.at[i])
+
+    chain_start(meta, zm_s, zm_r, 0)
+    load_x.wait()
+    chain_start(xg, zx_s, zx_r, 0)
+    load_g.wait()
+    chain_start(gg, zg_s, zg_r, 0)
     for i in range(3):
         w_copy(i).start()
-    load_g.wait()
     dispatch_x(z)
+    dispatch_g(z)
     for k in range(planes - 1):
         chain_wait(meta, zm_s, zm_r, k)
         chain_wait(xg, zx_s, zx_r, k)
         if k < planes - 2:
             chain_start(meta, zm_s, zm_r, k + 1)
             chain_start(xg, zx_s, zx_r, k + 1)
-        if k == planes - 3:
-            chain_start(gg, zg_s, zg_r, 0)
         both(dispatch_x, k)
-    dispatch_g(z)
-    chain_wait(gg, zg_s, zg_r, 0)
-    chain_start(gg, zg_s, zg_r, 1)
-    both(dispatch_g, 0)
-    for cp in load_w:
-        cp.wait()
-    for i in range(3):
-        w_copy(i).wait()
-    for p in range(planes):
-        plane_wait(st_x, rows, px_s, px_r, p)
-
-    def halves(src, dst, i):
-        lo = pl.ds(al(r * half, half), half)
-        hi = pl.ds(al(other * half, half), half)
-        return (
-            pltpu.make_async_copy(src.at[:, :, lo], dst.at[r], loc_sem.at[i]),
-            pltpu.make_async_remote_copy(
-                src_ref=src.at[:, :, hi], dst_ref=dst.at[r], send_sem=rep_s.at[i], recv_sem=rep_r.at[i],
-                device_id=(e, other), device_id_type=MESH),
-        )
-
-    rows_cp = halves(rows, rows_h, 0)
-    for cp in rows_cp:
-        cp.start()
-    step_h = 256 if hidden_n % 256 == 0 else hidden_n
-
-    @pl.loop(0, hidden_n // step_h)
-    def _(i):
-        cols = pl.ds(al(i * step_h, step_h), step_h)
-        a = rows[...].reshape(total, feat)
-        ga[:, cols] = jnp.dot(a, wg[:, cols], preferred_element_type=F32)
-        ua[:, cols] = jnp.dot(a, wu[:, cols], preferred_element_type=F32)
-
-    for k in range(1, planes - 1):
+        if k == 0:
+            for cp in load_w:
+                cp.wait()
+            for i in range(3):
+                w_copy(i).wait()
+            acts(z)
+        else:
+            both(acts, k - 1)
+        if k > 1:
+            forward_both(k - 2)
         chain_wait(gg, zg_s, zg_r, k)
         if k < planes - 2:
             chain_start(gg, zg_s, zg_r, k + 1)
         both(dispatch_g, k)
+        if k == 0:
+            grads(z)
+        else:
+            both(grads, k - 1)
+    both(acts, planes - 2)
+    forward_both(planes - 3)
+    both(grads, planes - 2)
+
     for p in range(planes):
-        plane_wait(st_g, scaled, pg_s, pg_r, p)
-    scaled_cp = halves(scaled, scaled_h, 1)
-    for cp in scaled_cp:
-        cp.start()
-
-    @pl.loop(0, hidden_n // step_h)
-    def _(i):
-        cols = pl.ds(al(i * step_h, step_h), step_h)
-        hg = lax.dot_general(scaled[...].reshape(total, feat), wd[cols, :], NT, preferred_element_type=F32)
-        gate_act, up_act = ga[:, cols], ua[:, cols]
-        sigma = jax.nn.sigmoid(gate_act)
-        silu = gate_act * sigma
-        hid[r, :, cols] = (silu * up_act).astype(BF16)
-        gate_gr[r, :, cols] = (hg * up_act * sigma * (1.0 + gate_act * (1.0 - sigma))).astype(BF16)
-        up_gr[r, :, cols] = (hg * silu).astype(BF16)
-
-    def rep_copy(ref, i):
-        return pltpu.make_async_remote_copy(
-            src_ref=ref.at[r], dst_ref=ref.at[r], send_sem=rep_s.at[i], recv_sem=rep_r.at[i],
-            device_id=(e, other), device_id_type=MESH)
-
-    rep_cp = [rep_copy(ref, 2 + i) for i, ref in enumerate((gate_gr, up_gr, hid))]
-    for cp in rep_cp:
-        cp.start()
-    step_d = 256
-
-    @pl.loop(0, feat // step_d)
-    def _(i):
-        cols = pl.ds(al(i * step_d, step_d), step_d)
-        v = lax.dot_general(gate_gr[r], wg[cols, :], NT, preferred_element_type=F32)
-        v = v + lax.dot_general(up_gr[r], wu[cols, :], NT, preferred_element_type=F32)
-        sg[:, :, cols] = v.astype(BF16).reshape(planes, slots, step_d)
-
-    order = sorted(range(planes), key=lambda p: min(p, last - p))
-    for p in order:
-        plane_send(sg, ret, pr_s, pr_r, p)
-
-    def part(p):
-        return jnp.dot(sel_t[p], ret[p], preferred_element_type=F32)
-
-    def ret_copy(way, p):
-        return pltpu.make_async_remote_copy(
-            src_ref=snd.at[p], dst_ref=rcv.at[way, p], send_sem=zr_s.at[p], recv_sem=zr_r.at[way, p],
-            device_id=(e + COLS if way == 0 else e - COLS, r), device_id_type=MESH)
-
-    def ret_wait(way, p):
-        pltpu.make_async_remote_copy(
-            src_ref=snd.at[p], dst_ref=rcv.at[way, p], send_sem=zr_s.at[p], recv_sem=zr_r.at[way, p],
-            device_id=(e, other), device_id_type=MESH).wait_recv()
-
-    def forward(way, p, first):
-        @pl.when(first)
-        def _():
-            snd[p] = part(p).astype(BF16)
-
-        @pl.when(jnp.logical_not(first))
-        def _():
-            ret_wait(way, p)
-            snd[p] = (part(p) + rcv[way, p].astype(F32)).astype(BF16)
-
-        ret_copy(way, p).start()
-
-    def weight_in(a_half, grads, out):
-        step = 256
-
-        @pl.loop(0, half // step)
-        def _(i):
-            cols = pl.ds(al(i * step, step), step)
-            v = lax.dot_general(a_half[0, :, :, cols].reshape(total, step), grads[0], TN, preferred_element_type=F32)
-            v = v + lax.dot_general(a_half[1, :, :, cols].reshape(total, step), grads[1], TN, preferred_element_type=F32)
-            out[0, cols, :] = v.astype(BF16)
-
-    def weight_down():
-        @pl.loop(0, hidden_n // step_h)
-        def _(i):
-            cols = pl.ds(al(i * step_h, step_h), step_h)
-            v = lax.dot_general(hid[0, :, cols], scaled_h[0].reshape(total, half), TN, preferred_element_type=F32)
-            v = v + lax.dot_general(hid[1, :, cols], scaled_h[1].reshape(total, half), TN, preferred_element_type=F32)
-            dwo_ref[0, cols, :] = v.astype(BF16)
-
-    for p in order:
-        plane_wait(sg, ret, pr_s, pr_r, p)
-    for k in range(planes):
-        @pl.when(k < z)
-        def _(k=k):
-            forward(1, k, z == last)
-
-        @pl.when(last - k > z)
-        def _(k=k):
-            forward(0, last - k, z == 0)
-
-        if k == 0:
-            for cp in (rows_cp, scaled_cp):
-                cp[0].wait()
-                cp[1].wait()
-            for cp in rep_cp:
+        for i, (src, dst) in enumerate(((rows, rows_h), (scaled, scaled_h))):
+            for cp in halves(src, dst, i, p):
                 cp.wait()
-            weight_in(rows_h, gate_gr, gwo_ref)
-        elif k == 1:
-            weight_in(rows_h, up_gr, uwo_ref)
-        elif k == 2:
-            weight_down()
-
-    own = part(z)
-    snd[z] = own.astype(BF16)
+        for i, ref in enumerate((gate_gr, up_gr, hid)):
+            rep_copy(ref, 2 + i, p).wait()
+    weight_in(rows_h, gate_gr, gwo_v)
+    out_copy(0).start()
+    forward_both(planes - 2)
+    weight_in(rows_h, up_gr, uwo_v)
+    out_copy(1).start()
+    weight_down()
+    out_copy(2).start()
+
+    plane_wait(sg, ret, pr_s, pr_r, z)
+    own_part[...] = jnp.dot(sel_t[z], ret[z], preferred_element_type=F32)
 
     @pl.when(z < last)
     def _():
-        ret_wait(1, z)
+        for q in range(PIECES):
+            ret_wait(1, z, q)
+        own_part[...] += rcv[1, z].astype(F32)
 
     @pl.when(z > 0)
     def _():
-        ret_wait(0, z)
-
-    above = jnp.where(z < last, rcv[1, z].astype(F32), 0.0)
-    below = jnp.where(z > 0, rcv[0, z].astype(F32), 0.0)
-    out_ref[...] = (own + above + below).astype(BF16)
+        for q in range(PIECES):
+            ret_wait(0, z, q)
+        own_part[...] += rcv[0, z].astype(F32)
+
+    out_ref[...] = own_part[...].astype(BF16)
+    for i in range(3):
+        out_copy(i).wait()
 
     chain_drain(meta, zm_s, zm_r)
     chain_drain(xg, zx_s, zx_r)
@@ -369,11 +393,13 @@
     for p in range(planes):
         @pl.when(p < z)
         def _(p=p):
-            ret_copy(1, p).wait_send()
+            for q in range(PIECES):
+                ret_copy(1, p, q).wait_send()
 
         @pl.when(p > z)
         def _(p=p):
-            ret_copy(0, p).wait_send()
+            for q in range(PIECES):
+                ret_copy(0, p, q).wait_send()
 
 
 def chained(inputs, out_grad, expert_ids, gates, gate_w, up_w, down_w):
@@ -388,24 +414,26 @@
     vmem = pl.BlockSpec(memory_space=pltpu.VMEM)
     hbm = pl.BlockSpec(memory_space=pl.ANY)
     block = (planes, slots, feat)
+    act = (planes, slots, hidden_n)
     scratch = [
         pltpu.VMEM((planes, tok, feat), BF16), pltpu.VMEM((planes, tok, feat), BF16),
         pltpu.VMEM((planes, 8, tok), F32),
         pltpu.VMEM(block, BF16), pltpu.VMEM(block, BF16), pltpu.VMEM(block, BF16), pltpu.VMEM(block, BF16),
         pltpu.VMEM((planes, tok, slots), BF16),
         pltpu.VMEM((feat, hidden_n), BF16), pltpu.VMEM((feat, hidden_n), BF16), pltpu.VMEM((hidden_n, feat), BF16),
-        pltpu.VMEM((total, hidden_n), F32), pltpu.VMEM((total, hidden_n), F32),
-        pltpu.VMEM((2, total, hidden_n), BF16), pltpu.VMEM((2, total, hidden_n), BF16),
-        pltpu.VMEM((2, total, hidden_n), BF16),
+        pltpu.VMEM(act, F32), pltpu.VMEM(act, F32),
+        pltpu.VMEM((2,) + act, BF16), pltpu.VMEM((2,) + act, BF16), pltpu.VMEM((2,) + act, BF16),
         pltpu.VMEM((2, planes, slots, half), BF16), pltpu.VMEM((2, planes, slots, half), BF16),
         pltpu.VMEM(block, BF16), pltpu.VMEM(block, BF16),
         pltpu.VMEM((2, planes, tok, feat), BF16), pltpu.VMEM((planes, tok, feat), BF16),
+        pltpu.VMEM((tok, feat), F32),
+        pltpu.VMEM(gate_w.shape, BF16), pltpu.VMEM(up_w.shape, BF16), pltpu.VMEM(down_w.shape, BF16),
         dma((5,)), dma((3,)), dma((3,)),
         dma((2, planes - 1)), dma((2, planes - 1)), dma((2, planes - 1)), dma((2, planes - 1)),
         dma((2, planes - 1)), dma((2, planes - 1)),
         dma((planes, COLS - 1)), dma((planes, COLS - 1)), dma((planes, COLS - 1)), dma((planes, COLS - 1)),
         dma((planes, COLS - 1)), dma((planes, COLS - 1)),
-        dma((planes,)), dma((2, planes)), dma((5,)), dma((5,)), dma((2,)),
+        dma((planes, PIECES)), dma((2, planes, PIECES)), dma((5, planes)), dma((5, planes)), dma((2, planes)), dma((3,)),
     ]
     return pl.pallas_call(
         functools.partial(layer_kernel, planes, experts, cap),
@@ -416,7 +444,7 @@
             jax.ShapeDtypeStruct(down_w.shape, BF16),
         ),
         in_specs=[vmem, vmem] + [hbm] * 5,
-        out_specs=(vmem,) * 4,
+        out_specs=(vmem, hbm, hbm, hbm),
         scratch_shapes=scratch,
         compiler_params=pltpu.CompilerParams(
             collective_id=0, has_side_effects=True, vmem_limit_bytes=60 * 1024 * 1024

time: 167 us -> 136 us (0.81)
  the two profiles are of different devices: /device:TPU:10 before, /device:TPU:0 now
where the time goes in v2:
time: 136 us
  Pallas kernels  127 us (93%)
  local copies, waits for them, and re-layouts  7.77 us (6%)
    pallas_call x1, Pallas kernels, chained(): pl.pallas_call(functools.partial(layer_kernel, planes, experts, cap), out...  127 us
    unnamed x8, local copies, waits for them, and re-layouts  7.77 us

profile of v2, /device:TPU:0, one launch (start us, length us, event | category | flops | bytes accessed | tf_op | source)
XLA Modules:
  0.0 135.6 jit_solution(5298923644225520292)
XLA Ops:
  0.6 127.2 %shard_map.102 = (bf16[128,2048]{1,0:T(8,128)(2,1)}, bf16[1,1024,768]{2,1,0:T(8,128)(2,1)}, bf16[1,1024,768]{2,1,0:T(8,128)(2,1)}, bf16[1,768,1024]{2,1,0:T(8,128)(2,1)}) custom-call(s32[2,128]{1,0:T(2,128)} %bitcast.2, f32[2,128]{1,0:T(2,128)} %bitcast.3, bf16[128,2048]{1,0:T(8,128)(2,1)} %x_hbm.1, bf16[128,2048]{1,0:T(8,128)(2,1)} %g_hbm.1, ...), custom_call_target="tpu_custom_call" | custom-call | flops 14495514624 | bytes 12582912 | tf_op jit(solution)/shard_map/pallas_call | solution.py:438
  127.8 1.9 %copy.15 = bf16[128,2048]{1,0:T(8,128)(2,1)} copy(bf16[128,2048]{1,0:T(8,128)(2,1)} %get-tuple-element.8) | data formatting | bytes 1048576
  129.7 0.0 copy-start.1
  129.7 2.8 %copy.16 = bf16[1,1024,768]{2,1,0:T(8,128)(2,1)} copy(bf16[1,1024,768]{2,1,0:T(8,128)(2,1)} %get-tuple-element.9) | data formatting | bytes 3145728
  132.5 0.0 copy-done.1
  132.5 0.0 copy-start
  132.5 1.1 copy.17
  133.6 0.8 copy-done
  134.4 1.1 copy.18
Async XLA Ops:
  129.7 2.8 %copy-start.1 = (bf16[1,1024,768]{2,1,0:T(8,128)(2,1)S(1)}, bf16[1,1024,768]{2,1,0:T(8,128)(2,1)}, u32[]{:S(2)}) copy-start(bf16[1,1024,768]{2,1,0:T(8,128)(2,1)} %get-tuple-element.10) | copy-start | bytes 4718596
  132.5 2.0 %copy-start = (bf16[1,768,1024]{2,1,0:T(8,128)(2,1)S(1)}, bf16[1,768,1024]{2,1,0:T(8,128)(2,1)}, u32[]{:S(2)}) copy-start(bf16[1,768,1024]{2,1,0:T(8,128)(2,1)} %get-tuple-element.11) | copy-start | bytes 4718596

commit v3 on v2

--- a/solution.py
+++ b/solution.py
@@ -322,6 +322,11 @@
         w_copy(i).start()
     dispatch_x(z)
     dispatch_g(z)
+    for cp in load_w:
+        cp.wait()
+    for i in range(3):
+        w_copy(i).wait()
+    acts(z)
     for k in range(planes - 1):
         chain_wait(meta, zm_s, zm_r, k)
         chain_wait(xg, zx_s, zx_r, k)
@@ -330,40 +335,40 @@
             chain_start(xg, zx_s, zx_r, k + 1)
         both(dispatch_x, k)
         if k == 0:
-            for cp in load_w:
-                cp.wait()
-            for i in range(3):
-                w_copy(i).wait()
-            acts(z)
+            grads(z)
         else:
-            both(acts, k - 1)
-        if k > 1:
-            forward_both(k - 2)
+            both(grads, k - 1)
         chain_wait(gg, zg_s, zg_r, k)
         if k < planes - 2:
             chain_start(gg, zg_s, zg_r, k + 1)
         both(dispatch_g, k)
-        if k == 0:
-            grads(z)
-        else:
-            both(grads, k - 1)
-    both(acts, planes - 2)
-    forward_both(planes - 3)
+        both(acts, k)
+        if k > 0:
+            forward_both(k - 1)
     both(grads, planes - 2)
 
-    for p in range(planes):
-        for i, (src, dst) in enumerate(((rows, rows_h), (scaled, scaled_h))):
-            for cp in halves(src, dst, i, p):
-                cp.wait()
-        for i, ref in enumerate((gate_gr, up_gr, hid)):
-            rep_copy(ref, 2 + i, p).wait()
-    weight_in(rows_h, gate_gr, gwo_v)
-    out_copy(0).start()
-    forward_both(planes - 2)
-    weight_in(rows_h, up_gr, uwo_v)
-    out_copy(1).start()
-    weight_down()
-    out_copy(2).start()
+    is_end = jnp.where((z == 0) | (z == last), 1, 0)
+
+    @pl.loop(0, 2)
+    def _(phase):
+        @pl.when(phase == is_end)
+        def _():
+            for p in range(planes):
+                for i, (src, dst) in enumerate(((rows, rows_h), (scaled, scaled_h))):
+                    for cp in halves(src, dst, i, p):
+                        cp.wait()
+                for i, ref in enumerate((gate_gr, up_gr, hid)):
+                    rep_copy(ref, 2 + i, p).wait()
+            weight_in(rows_h, gate_gr, gwo_v)
+            out_copy(0).start()
+            weight_in(rows_h, up_gr, uwo_v)
+            out_copy(1).start()
+            weight_down()
+            out_copy(2).start()
+
+        @pl.when(phase == 0)
+        def _():
+            forward_both(planes - 2)
 
     plane_wait(sg, ret, pr_s, pr_r, z)
     own_part[...] = jnp.dot(sel_t[z], ret[z], preferred_element_type=F32)
@@ -400,6 +405,22 @@
         def _(p=p):
             for q in range(PIECES):
                 ret_copy(0, p, q).wait_send()
+
+
+def hand_over(*refs):
+    count = len(refs) // 2
+    srcs, dsts, sem = refs[:count], refs[count : 2 * count], refs[2 * count]
+    copies = []
+    for i in range(count):
+        axis = len(srcs[i].shape) - 2
+        piece = srcs[i].shape[axis] // PIECES
+        for q in range(PIECES):
+            at = (0,) * axis + (pl.ds(q * piece, piece),)
+            copies.append(pltpu.make_async_copy(srcs[i].at[at], dsts[i].at[at], sem.at[i, q]))
+    for cp in copies:
+        cp.start()
+    for cp in copies:
+        cp.wait()
 
 
 def chained(inputs, out_grad, expert_ids, gates, gate_w, up_w, down_w):
@@ -435,7 +456,7 @@
         dma((planes, COLS - 1)), dma((planes, COLS - 1)),
         dma((planes, PIECES)), dma((2, planes, PIECES)), dma((5, planes)), dma((5, planes)), dma((2, planes)), dma((3,)),
     ]
-    return pl.pallas_call(
+    results = pl.pallas_call(
         functools.partial(layer_kernel, planes, experts, cap),
         out_shape=(
             jax.ShapeDtypeStruct((tok, feat), BF16),
@@ -453,6 +474,13 @@
             flops=18 * total * feat * hidden_n, bytes_accessed=8 * feat * hidden_n, transcendentals=total * hidden_n
         ),
     )(expert_ids.T, gates.T, inputs, out_grad, gate_w, up_w, down_w)
+    return pl.pallas_call(
+        hand_over,
+        out_shape=tuple(jax.ShapeDtypeStruct(a.shape, a.dtype) for a in results),
+        in_specs=[hbm] * 4,
+        out_specs=(hbm,) * 4,
+        scratch_shapes=[dma((4, PIECES))],
+    )(*results)
 
 
 def arrange(received, owners, local_exp, capacity):

time: 136 us -> 281 us (2.07)
  Pallas kernels: 127 us -> 280 us
  local copies, waits for them, and re-layouts: 7.77 us -> 0 us
    pallas_call x0 -> x1, Pallas kernels: none -> 160 us  [chained(): pl.pallas_call(hand_over, out_shape=tuple((jax.ShapeDtypeStruct(a.shape,...]
    unnamed x8 -> x0, local copies, waits for them, and re-layouts: 7.77 us -> none
    pallas_call x1, Pallas kernels: 127 us -> 120 us  [chained(): pl.pallas_call(functools.partial(layer_kernel, planes, experts, cap), out...]
where the time goes in v3:
time: 281 us
  Pallas kernels  280 us (100%)
    pallas_call x1, Pallas kernels, chained(): pl.pallas_call(hand_over, out_shape=tuple((jax.ShapeDtypeStruct(a.shape,...  160 us
    pallas_call x1, Pallas kernels, chained(): pl.pallas_call(functools.partial(layer_kernel, planes, experts, cap), out...  120 us

profile of v3, /device:TPU:0, one launch (start us, length us, event | category | flops | bytes accessed | tf_op | source)
XLA Modules:
  0.0 281.1 jit_solution(17591368066863522568)
XLA Ops:
  0.6 120.2 %shard_map.102 = (bf16[128,2048]{1,0:T(8,128)(2,1)}, bf16[1,1024,768]{2,1,0:T(8,128)(2,1)}, bf16[1,1024,768]{2,1,0:T(8,128)(2,1)}, bf16[1,768,1024]{2,1,0:T(8,128)(2,1)}) custom-call(s32[2,128]{1,0:T(2,128)} %bitcast.2, f32[2,128]{1,0:T(2,128)} %bitcast.3, bf16[128,2048]{1,0:T(8,128)(2,1)} %x_hbm.1, bf16[128,2048]{1,0:T(8,128)(2,1)} %g_hbm.1, ...), custom_call_target="tpu_custom_call" | custom-call | flops 14495514624 | bytes 12582912 | tf_op jit(solution)/shard_map/pallas_call | solution.py:459
  120.8 160.1 %shard_map.103 = (bf16[128,2048]{1,0:T(8,128)(2,1)}, bf16[1,1024,768]{2,1,0:T(8,128)(2,1)}, bf16[1,1024,768]{2,1,0:T(8,128)(2,1)}, bf16[1,768,1024]{2,1,0:T(8,128)(2,1)}) custom-call(bf16[128,2048]{1,0:T(8,128)(2,1)} %get-tuple-element.8.refs_0_, bf16[1,1024,768]{2,1,0:T(8,128)(2,1)} %get-tuple-element.9.refs_1_, ...), custom_call_target="tpu_custom_call" | custom-call | tf_op jit(solution)/shard_map/pallas_call | solution.py:477

commit v4 on v3

--- a/solution.py
+++ b/solution.py
@@ -10,6 +10,7 @@
 MESH = pl.DeviceIdType.MESH
 COLS = 4
 PIECES = 4
+GPARTS = 2
 F32 = jnp.float32
 BF16 = jnp.bfloat16
 NT = (((1,), (1,)), ((), ()))
@@ -22,7 +23,7 @@
     out_ref, gwo_ref, uwo_ref, dwo_ref,
     xg, gg, meta, st_x, st_g, rows, scaled, sel_t, wg, wu, wd, ga, ua,
     hid, gate_gr, up_gr, rows_h, scaled_h, sg, ret, rcv, snd,
-    own_part, gwo_v, uwo_v, dwo_v,
+    own_part, hg_part, gwo_v, uwo_v, dwo_v,
     load_sem, w_send, w_recv, zm_s, zm_r, zx_s, zx_r, zg_s, zg_r,
     px_s, px_r, pg_s, pg_r, pr_s, pr_r, zr_s, zr_r, rep_s, rep_r, loc_sem, out_sem,
 ):
@@ -82,15 +83,27 @@
     neighbours = COLS + jnp.where(z < last, 1, 0) + jnp.where(z > 0, 1, 0)
     pl.semaphore_wait(barrier, neighbours)
 
-    def up(buf, ss, rs, k):
+    def span(part):
+        wide = feat // GPARTS
+        return (slice(None), pl.ds(part * wide, wide))
+
+    def at_part(ref, i, part):
+        return ref.at[i] if part is None else ref.at[(i,) + span(part)]
+
+    def at_sem(sem, way, k, part):
+        return sem.at[way, k] if part is None else sem.at[way, k, part]
+
+    def chain_copy(buf, ss, rs, way, k, part, i, target):
         return pltpu.make_async_remote_copy(
-            src_ref=buf.at[jnp.maximum(z - k, 0)], dst_ref=buf.at[jnp.maximum(z - k, 0)],
-            send_sem=ss.at[0, k], recv_sem=rs.at[0, k], device_id=(e + COLS, r), device_id_type=MESH)
-
-    def down(buf, ss, rs, k):
-        return pltpu.make_async_remote_copy(
-            src_ref=buf.at[jnp.minimum(z + k, last)], dst_ref=buf.at[jnp.minimum(z + k, last)],
-            send_sem=ss.at[1, k], recv_sem=rs.at[1, k], device_id=(e - COLS, r), device_id_type=MESH)
+            src_ref=at_part(buf, i, part), dst_ref=at_part(buf, i, part),
+            send_sem=at_sem(ss, way, k, part), recv_sem=at_sem(rs, way, k, part),
+            device_id=target, device_id_type=MESH)
+
+    def up(buf, ss, rs, k, part):
+        return chain_copy(buf, ss, rs, 0, k, part, jnp.maximum(z - k, 0), (e + COLS, r))
+
+    def down(buf, ss, rs, k, part):
+        return chain_copy(buf, ss, rs, 1, k, part, jnp.minimum(z + k, last), (e - COLS, r))
 
     def can_up(k):
         return (z < last) & (z - k >= 0)
@@ -98,61 +111,59 @@
     def can_down(k):
         return (z > 0) & (z + k <= last)
 
-    def chain_start(buf, ss, rs, k):
+    def chain_start(buf, ss, rs, k, part=None):
         @pl.when(can_up(k))
         def _():
-            up(buf, ss, rs, k).start()
+            up(buf, ss, rs, k, part).start()
 
         @pl.when(can_down(k))
         def _():
-            down(buf, ss, rs, k).start()
-
-    def chain_wait(buf, ss, rs, k):
+            down(buf, ss, rs, k, part).start()
+
+    def chain_wait(buf, ss, rs, k, part=None):
         @pl.when(z - 1 - k >= 0)
         def _():
-            b = buf.at[jnp.maximum(z - 1 - k, 0)]
-            pltpu.make_async_remote_copy(
-                src_ref=b, dst_ref=b, send_sem=ss.at[0, k], recv_sem=rs.at[0, k],
-                device_id=(e, other), device_id_type=MESH).wait_recv()
+            chain_copy(buf, ss, rs, 0, k, part, jnp.maximum(z - 1 - k, 0), (e, other)).wait_recv()
 
         @pl.when(z + 1 + k <= last)
         def _():
-            b = buf.at[jnp.minimum(z + 1 + k, last)]
-            pltpu.make_async_remote_copy(
-                src_ref=b, dst_ref=b, send_sem=ss.at[1, k], recv_sem=rs.at[1, k],
-                device_id=(e, other), device_id_type=MESH).wait_recv()
-
-    def chain_drain(buf, ss, rs):
+            chain_copy(buf, ss, rs, 1, k, part, jnp.minimum(z + 1 + k, last), (e, other)).wait_recv()
+
+    def chain_drain(buf, ss, rs, parts=(None,)):
         for k in range(planes - 1):
-            @pl.when(can_up(k))
-            def _(k=k):
-                up(buf, ss, rs, k).wait_send()
-
-            @pl.when(can_down(k))
-            def _(k=k):
-                down(buf, ss, rs, k).wait_send()
-
-    def plane_copy(st, dst, ss, rs, p, j):
+            for part in parts:
+                @pl.when(can_up(k))
+                def _(k=k, part=part):
+                    up(buf, ss, rs, k, part).wait_send()
+
+                @pl.when(can_down(k))
+                def _(k=k, part=part):
+                    down(buf, ss, rs, k, part).wait_send()
+
+    def plane_copy(st, dst, ss, rs, p, j, q, parts):
         d = (c + j) % COLS
+        cols = pl.ds(al(q * (feat // parts), feat // parts), feat // parts)
         return pltpu.make_async_remote_copy(
-            src_ref=st.at[p, pl.ds(al(d * cap, cap), cap)],
-            dst_ref=dst.at[p, pl.ds(al(c * cap, cap), cap)],
-            send_sem=ss.at[p, j - 1], recv_sem=rs.at[p, j - 1],
+            src_ref=st.at[p, pl.ds(al(d * cap, cap), cap), cols],
+            dst_ref=dst.at[p, pl.ds(al(c * cap, cap), cap), cols],
+            send_sem=ss.at[p, j - 1, q], recv_sem=rs.at[p, j - 1, q],
             device_id=(z * COLS + d, r), device_id_type=MESH)
 
-    def plane_send(st, dst, ss, rs, p):
+    def plane_send(st, dst, ss, rs, p, q=0, parts=1):
         for j in range(1, COLS):
-            plane_copy(st, dst, ss, rs, p, j).start()
-        dst[p, pl.ds(al(c * cap, cap), cap), :] = st[p, pl.ds(al(c * cap, cap), cap), :]
-
-    def plane_wait(st, dst, ss, rs, p):
+            plane_copy(st, dst, ss, rs, p, j, q, parts).start()
+        cols = pl.ds(al(q * (feat // parts), feat // parts), feat // parts)
+        dst[p, pl.ds(al(c * cap, cap), cap), cols] = st[p, pl.ds(al(c * cap, cap), cap), cols]
+
+    def plane_wait(st, dst, ss, rs, p, q=0, parts=1):
         for j in range(1, COLS):
-            plane_copy(st, dst, ss, rs, p, j).wait_recv()
-
-    def plane_drain(st, dst, ss, rs):
+            plane_copy(st, dst, ss, rs, p, j, q, parts).wait_recv()
+
+    def plane_drain(st, dst, ss, rs, parts=1):
         for p in range(planes):
             for j in range(1, COLS):
-                plane_copy(st, dst, ss, rs, p, j).wait_send()
+                for q in range(parts):
+                    plane_copy(st, dst, ss, rs, p, j, q, parts).wait_send()
 
     def selection(p):
         m = meta[p]
@@ -166,12 +177,13 @@
         st_x[p] = jnp.dot(pick.astype(BF16), xg[p], preferred_element_type=F32).astype(BF16)
         plane_send(st_x, rows, px_s, px_r, p)
 
-    def dispatch_g(p):
+    def dispatch_g(p, part):
         s0, s1, m = selection(p)
         gate = jnp.sum(s0 * m[2:3, :] + s1 * m[3:4, :], axis=1, keepdims=True)
-        picked = jnp.dot((s0 + s1).astype(BF16), gg[p], preferred_element_type=F32)
-        st_g[p] = (picked * gate).astype(BF16)
-        plane_send(st_g, scaled, pg_s, pg_r, p)
+        at = (p,) + span(part)
+        picked = jnp.dot((s0 + s1).astype(BF16), gg[at], preferred_element_type=F32)
+        st_g[at] = (picked * gate).astype(BF16)
+        plane_send(st_g, scaled, pg_s, pg_r, p, part, GPARTS)
 
     def both(fn, k):
         @pl.when(z - 1 - k >= 0)
@@ -204,7 +216,7 @@
             device_id=(e, other), device_id_type=MESH)
 
     step_h = 256 if hidden_n % 256 == 0 else hidden_n
-    step_d = 512
+    step_d = feat // PIECES
 
     def acts(p):
         plane_wait(st_x, rows, px_s, px_r, p)
@@ -218,60 +230,71 @@
             ua[p, :, cols] = jnp.dot(rows[p], wu[:, cols], preferred_element_type=F32)
 
     def grads(p):
-        plane_wait(st_g, scaled, pg_s, pg_r, p)
-        for cp in halves(scaled, scaled_h, 1, p):
-            cp.start()
-
-        @pl.loop(0, hidden_n // step_h)
-        def _(i):
-            cols = pl.ds(al(i * step_h, step_h), step_h)
-            hg = lax.dot_general(scaled[p], wd[cols, :], NT, preferred_element_type=F32)
-            gate_act, up_act = ga[p, :, cols], ua[p, :, cols]
-            sigma = jax.nn.sigmoid(gate_act)
-            silu = gate_act * sigma
-            hid[r, p, :, cols] = (silu * up_act).astype(BF16)
-            gate_gr[r, p, :, cols] = (hg * up_act * sigma * (1.0 + gate_act * (1.0 - sigma))).astype(BF16)
-            up_gr[r, p, :, cols] = (hg * silu).astype(BF16)
-
-        @pl.loop(0, feat // step_d)
+        for part in range(GPARTS):
+            plane_wait(st_g, scaled, pg_s, pg_r, p, part, GPARTS)
+            at = span(part)
+
+            @pl.loop(0, hidden_n // step_h)
+            def _(i):
+                cols = pl.ds(al(i * step_h, step_h), step_h)
+                hg = lax.dot_general(scaled[(p,) + at], wd[cols, at[1]], NT, preferred_element_type=F32)
+                if part < GPARTS - 1:
+                    hg_part[:, cols] = hg if part == 0 else hg_part[:, cols] + hg
+                else:
+                    if part > 0:
+                        hg = hg + hg_part[:, cols]
+                    gate_act, up_act = ga[p, :, cols], ua[p, :, cols]
+                    sigma = jax.nn.sigmoid(gate_act)
+                    silu = gate_act * sigma
+                    hid[r, p, :, cols] = (silu * up_act).astype(BF16)
+                    gate_gr[r, p, :, cols] = (hg * up_act * sigma * (1.0 + gate_act * (1.0 - sigma))).astype(BF16)
+                    up_gr[r, p, :, cols] = (hg * silu).astype(BF16)
+
+        @pl.loop(0, PIECES)
         def _(i):
             cols = pl.ds(al(i * step_d, step_d), step_d)
             v = lax.dot_general(gate_gr[r, p], wg[cols, :], NT, preferred_element_type=F32)
             v = v + lax.dot_general(up_gr[r, p], wu[cols, :], NT, preferred_element_type=F32)
             sg[p, :, cols] = v.astype(BF16)
-
-        plane_send(sg, ret, pr_s, pr_r, p)
+            plane_send(sg, ret, pr_s, pr_r, p, i, PIECES)
+
         for i, ref in enumerate((gate_gr, up_gr, hid)):
             rep_copy(ref, 2 + i, p).start()
-
-    piece = tok // PIECES
+        for cp in halves(scaled, scaled_h, 1, p):
+            cp.start()
+
+    def piece(q):
+        return pl.ds(al(q * step_d, step_d), step_d)
 
     def ret_copy(way, p, q):
-        at = pl.ds(q * piece, piece)
         return pltpu.make_async_remote_copy(
-            src_ref=snd.at[p, at], dst_ref=rcv.at[way, p, at], send_sem=zr_s.at[p, q], recv_sem=zr_r.at[way, p, q],
+            src_ref=snd.at[p, :, piece(q)], dst_ref=rcv.at[way, p, :, piece(q)],
+            send_sem=zr_s.at[p, q], recv_sem=zr_r.at[way, p, q],
             device_id=(jnp.where(way == 0, e + COLS, e - COLS), r), device_id_type=MESH)
 
     def ret_wait(way, p, q):
-        at = pl.ds(q * piece, piece)
         pltpu.make_async_remote_copy(
-            src_ref=snd.at[p, at], dst_ref=rcv.at[way, p, at], send_sem=zr_s.at[p, q], recv_sem=zr_r.at[way, p, q],
+            src_ref=snd.at[p, :, piece(q)], dst_ref=rcv.at[way, p, :, piece(q)],
+            send_sem=zr_s.at[p, q], recv_sem=zr_r.at[way, p, q],
             device_id=(e, other), device_id_type=MESH).wait_recv()
 
+    def own_sum(p, q):
+        plane_wait(sg, ret, pr_s, pr_r, p, q, PIECES)
+        return jnp.dot(sel_t[p], ret[p, :, piece(q)], preferred_element_type=F32)
+
     def forward(way, p, first):
-        plane_wait(sg, ret, pr_s, pr_r, p)
-        own_part[...] = jnp.dot(sel_t[p], ret[p], preferred_element_type=F32)
-        for q in range(PIECES):
-            at = pl.ds(q * piece, piece)
+        @pl.loop(0, PIECES)
+        def _(q):
+            own = own_sum(p, q)
 
             @pl.when(first)
             def _():
-                snd[p, at, :] = own_part[at, :].astype(BF16)
+                snd[p, :, piece(q)] = own.astype(BF16)
 
             @pl.when(jnp.logical_not(first))
             def _():
                 ret_wait(way, p, q)
-                snd[p, at, :] = (own_part[at, :] + rcv[way, p, at, :].astype(F32)).astype(BF16)
+                snd[p, :, piece(q)] = (own + rcv[way, p, :, piece(q)].astype(F32)).astype(BF16)
 
             ret_copy(way, p, q).start()
 
@@ -317,11 +340,13 @@
     load_x.wait()
     chain_start(xg, zx_s, zx_r, 0)
     load_g.wait()
-    chain_start(gg, zg_s, zg_r, 0)
+    for part in range(GPARTS):
+        chain_start(gg, zg_s, zg_r, 0, part)
     for i in range(3):
         w_copy(i).start()
     dispatch_x(z)
-    dispatch_g(z)
+    for part in range(GPARTS):
+        dispatch_g(z, part)
     for cp in load_w:
         cp.wait()
     for i in range(3):
@@ -338,10 +363,11 @@
             grads(z)
         else:
             both(grads, k - 1)
-        chain_wait(gg, zg_s, zg_r, k)
-        if k < planes - 2:
-            chain_start(gg, zg_s, zg_r, k + 1)
-        both(dispatch_g, k)
+        for part in range(GPARTS):
+            chain_wait(gg, zg_s, zg_r, k, part)
+            if k < planes - 2:
+                chain_start(gg, zg_s, zg_r, k + 1, part)
+            both(functools.partial(dispatch_g, part=part), k)
         both(acts, k)
         if k > 0:
             forward_both(k - 1)
@@ -370,31 +396,31 @@
         def _():
             forward_both(planes - 2)
 
-    plane_wait(sg, ret, pr_s, pr_r, z)
-    own_part[...] = jnp.dot(sel_t[z], ret[z], preferred_element_type=F32)
-
-    @pl.when(z < last)
-    def _():
-        for q in range(PIECES):
+    @pl.loop(0, PIECES)
+    def _(q):
+        own_part[...] = own_sum(z, q)
+
+        @pl.when(z < last)
+        def _():
             ret_wait(1, z, q)
-        own_part[...] += rcv[1, z].astype(F32)
-
-    @pl.when(z > 0)
-    def _():
-        for q in range(PIECES):
+            own_part[...] += rcv[1, z, :, piece(q)].astype(F32)
+
+        @pl.when(z > 0)
+        def _():
             ret_wait(0, z, q)
-        own_part[...] += rcv[0, z].astype(F32)
-
-    out_ref[...] = own_part[...].astype(BF16)
+            own_part[...] += rcv[0, z, :, piece(q)].astype(F32)
+
+        out_ref[:, piece(q)] = own_part[...].astype(BF16)
+
     for i in range(3):
         out_copy(i).wait()
 
     chain_drain(meta, zm_s, zm_r)
     chain_drain(xg, zx_s, zx_r)
-    chain_drain(gg, zg_s, zg_r)
+    chain_drain(gg, zg_s, zg_r, range(GPARTS))
     plane_drain(st_x, rows, px_s, px_r)
-    plane_drain(st_g, scaled, pg_s, pg_r)
-    plane_drain(sg, ret, pr_s, pr_r)
+    plane_drain(st_g, scaled, pg_s, pg_r, GPARTS)
+    plane_drain(sg, ret, pr_s, pr_r, PIECES)
     for p in range(planes):
         @pl.when(p < z)
         def _(p=p):
@@ -408,18 +434,21 @@
 
 
 def hand_over(*refs):
-    count = len(refs) // 2
-    srcs, dsts, sem = refs[:count], refs[count : 2 * count], refs[2 * count]
-    copies = []
-    for i in range(count):
+    srcs, dsts, held, sems = refs[:4], refs[4:8], refs[8:12], refs[12]
+    loads, stores = [], []
+    for i in range(4):
         axis = len(srcs[i].shape) - 2
         piece = srcs[i].shape[axis] // PIECES
         for q in range(PIECES):
             at = (0,) * axis + (pl.ds(q * piece, piece),)
-            copies.append(pltpu.make_async_copy(srcs[i].at[at], dsts[i].at[at], sem.at[i, q]))
-    for cp in copies:
+            loads.append(pltpu.make_async_copy(srcs[i].at[at], held[i].at[at], sems.at[0, i, q]))
+            stores.append(pltpu.make_async_copy(held[i].at[at], dsts[i].at[at], sems.at[1, i, q]))
+    for cp in loads:
         cp.start()
-    for cp in copies:
+    for load, store in zip(loads, stores):
+        load.wait()
+        store.start()
+    for cp in stores:
         cp.wait()
 
 
@@ -447,13 +476,14 @@
         pltpu.VMEM((2, planes, slots, half), BF16), pltpu.VMEM((2, planes, slots, half), BF16),
         pltpu.VMEM(block, BF16), pltpu.VMEM(block, BF16),
         pltpu.VMEM((2, planes, tok, feat), BF16), pltpu.VMEM((planes, tok, feat), BF16),
-        pltpu.VMEM((tok, feat), F32),
+        pltpu.VMEM((tok, feat // PIECES), F32), pltpu.VMEM((slots, hidden_n), F32),
         pltpu.VMEM(gate_w.shape, BF16), pltpu.VMEM(up_w.shape, BF16), pltpu.VMEM(down_w.shape, BF16),
         dma((5,)), dma((3,)), dma((3,)),
         dma((2, planes - 1)), dma((2, planes - 1)), dma((2, planes - 1)), dma((2, planes - 1)),
-        dma((2, planes - 1)), dma((2, planes - 1)),
-        dma((planes, COLS - 1)), dma((planes, COLS - 1)), dma((planes, COLS - 1)), dma((planes, COLS - 1)),
-        dma((planes, COLS - 1)), dma((planes, COLS - 1)),
+        dma((2, planes - 1, GPARTS)), dma((2, planes - 1, GPARTS)),
+        dma((planes, COLS - 1, 1)), dma((planes, COLS - 1, 1)),
+        dma((planes, COLS - 1, GPARTS)), dma((planes, COLS - 1, GPARTS)),
+        dma((planes, COLS - 1, PIECES)), dma((planes, COLS - 1, PIECES)),
         dma((planes, PIECES)), dma((2, planes, PIECES)), dma((5, planes)), dma((5, planes)), dma((2, planes)), dma((3,)),
     ]
     results = pl.pallas_call(
@@ -479,7 +509,8 @@
         out_shape=tuple(jax.ShapeDtypeStruct(a.shape, a.dtype) for a in results),
         in_specs=[hbm] * 4,
         out_specs=(hbm,) * 4,
-        scratch_shapes=[dma((4, PIECES))],
+        scratch_shapes=[pltpu.VMEM(a.shape, a.dtype) for a in results] + [dma((2, 4, PIECES))],
+        compiler_params=pltpu.CompilerParams(vmem_limit_bytes=16 * 1024 * 1024),
     )(*results)
 
 

time: 281 us -> 129 us (0.46)
  Pallas kernels: 280 us -> 122 us
  local copies, waits for them, and re-layouts: 0 us -> 5.26 us
    pallas_call x1, Pallas kernels: 160 us -> 5.49 us  [chained(): pl.pallas_call(hand_over, out_shape=tuple((jax.ShapeDtypeStruct(a.shape,...]
    unnamed x0 -> x8, local copies, waits for them, and re-layouts: none -> 5.26 us
    pallas_call x1, Pallas kernels: 120 us -> 117 us  [chained(): pl.pallas_call(functools.partial(layer_kernel, planes, experts, cap), out...]
where the time goes in v4:
time: 129 us; the launch traced here: 128 us
  Pallas kernels  122 us (95%)
  local copies, waits for them, and re-layouts  5.26 us (4%)
    pallas_call x1, Pallas kernels, chained(): pl.pallas_call(functools.partial(layer_kernel, planes, experts, cap), out...  117 us
    pallas_call x1, Pallas kernels, chained(): pl.pallas_call(hand_over, out_shape=tuple((jax.ShapeDtypeStruct(a.shape,...  5.49 us
    unnamed x8, local copies, waits for them, and re-layouts  5.26 us

profile of v4, /device:TPU:0, one launch (start us, length us, event | category | flops | bytes accessed | tf_op | source)
XLA Modules:
  0.0 128.3 jit_solution(15537178790655013315)
XLA Ops:
  0.6 116.7 %shard_map.102 = (bf16[128,2048]{1,0:T(8,128)(2,1)}, bf16[1,1024,768]{2,1,0:T(8,128)(2,1)}, bf16[1,1024,768]{2,1,0:T(8,128)(2,1)}, bf16[1,768,1024]{2,1,0:T(8,128)(2,1)}) custom-call(s32[2,128]{1,0:T(2,128)} %bitcast.2, f32[2,128]{1,0:T(2,128)} %bitcast.3, bf16[128,2048]{1,0:T(8,128)(2,1)} %x_hbm.1, bf16[128,2048]{1,0:T(8,128)(2,1)} %g_hbm.1, ...), custom_call_target="tpu_custom_call" | custom-call | flops 14495514624 | bytes 12582912 | tf_op jit(solution)/shard_map/pallas_call | solution.py:489
  117.4 0.0 copy-start
  117.4 1.4 %copy-done = bf16[1,1024,768]{2,1,0:T(8,128)(2,1)S(1)} copy-done((bf16[1,1024,768]{2,1,0:T(8,128)(2,1)S(1)}, bf16[1,1024,768]{2,1,0:T(8,128)(2,1)}, u32[]{:S(2)}) %copy-start) | copy-done | bytes 1572888
  118.8 0.0 copy-start.1
  118.8 1.4 %copy-done.1 = bf16[1,1024,768]{2,1,0:T(8,128)(2,1)S(1)} copy-done((bf16[1,1024,768]{2,1,0:T(8,128)(2,1)S(1)}, bf16[1,1024,768]{2,1,0:T(8,128)(2,1)}, u32[]{:S(2)}) %copy-start.1) | copy-done | bytes 1572888
  120.2 0.0 copy-start.2
  120.2 1.4 %copy-done.2 = bf16[1,768,1024]{2,1,0:T(8,128)(2,1)S(1)} copy-done((bf16[1,768,1024]{2,1,0:T(8,128)(2,1)S(1)}, bf16[1,768,1024]{2,1,0:T(8,128)(2,1)}, u32[]{:S(2)}) %copy-start.2) | copy-done | bytes 1572888
  121.6 0.0 copy-start.3
  121.6 1.0 copy-done.3
  122.7 5.5 %shard_map.103 = (bf16[128,2048]{1,0:T(8,128)(2,1)}, bf16[1,1024,768]{2,1,0:T(8,128)(2,1)}, bf16[1,1024,768]{2,1,0:T(8,128)(2,1)}, bf16[1,768,1024]{2,1,0:T(8,128)(2,1)}) custom-call(bf16[128,2048]{1,0:T(8,128)(2,1)S(1)} %copy-done.3, bf16[1,1024,768]{2,1,0:T(8,128)(2,1)S(1)} %copy-done, bf16[1,1024,768]{2,1,0:T(8,128)(2,1)S(1)} %copy-done.1, ...), custom_call_target="tpu_custom_call" | custom-call | tf_op jit(solution)/shard_map/pallas_call | solution.py:507
Async XLA Ops:
  117.4 1.4 %copy-start = (bf16[1,1024,768]{2,1,0:T(8,128)(2,1)S(1)}, bf16[1,1024,768]{2,1,0:T(8,128)(2,1)}, u32[]{:S(2)}) copy-start(bf16[1,1024,768]{2,1,0:T(8,128)(2,1)} %get-tuple-element.9.refs_1_) | copy-start | bytes 4718596
  118.8 1.4 %copy-start.1 = (bf16[1,1024,768]{2,1,0:T(8,128)(2,1)S(1)}, bf16[1,1024,768]{2,1,0:T(8,128)(2,1)}, u32[]{:S(2)}) copy-start(bf16[1,1024,768]{2,1,0:T(8,128)(2,1)} %get-tuple-element.10.refs_2_) | copy-start | bytes 4718596
  120.2 1.4 %copy-start.2 = (bf16[1,768,1024]{2,1,0:T(8,128)(2,1)S(1)}, bf16[1,768,1024]{2,1,0:T(8,128)(2,1)}, u32[]{:S(2)}) copy-start(bf16[1,768,1024]{2,1,0:T(8,128)(2,1)} %get-tuple-element.11.refs_3_) | copy-start | bytes 4718596
  121.6 1.0 copy-start.3

commit v5 on v4

--- a/solution.py
+++ b/solution.py
@@ -336,16 +336,31 @@
         src, dst = ((gwo_v, gwo_ref), (uwo_v, uwo_ref), (dwo_v, dwo_ref))[i]
         return pltpu.make_async_copy(src, dst, out_sem.at[i])
 
+    def weight_grads():
+        @pl.loop(0, planes)
+        def _(p):
+            for i, (src, dst) in enumerate(((rows, rows_h), (scaled, scaled_h))):
+                for cp in halves(src, dst, i, p):
+                    cp.wait()
+            for i, ref in enumerate((gate_gr, up_gr, hid)):
+                rep_copy(ref, 2 + i, p).wait()
+
+        weight_in(rows_h, gate_gr, gwo_v)
+        out_copy(0).start()
+        weight_in(rows_h, up_gr, uwo_v)
+        out_copy(1).start()
+        weight_down()
+        out_copy(2).start()
+
     chain_start(meta, zm_s, zm_r, 0)
     load_x.wait()
     chain_start(xg, zx_s, zx_r, 0)
     load_g.wait()
-    for part in range(GPARTS):
-        chain_start(gg, zg_s, zg_r, 0, part)
     for i in range(3):
         w_copy(i).start()
     dispatch_x(z)
     for part in range(GPARTS):
+        chain_start(gg, zg_s, zg_r, 0, part)
         dispatch_g(z, part)
     for cp in load_w:
         cp.wait()
@@ -363,38 +378,28 @@
             grads(z)
         else:
             both(grads, k - 1)
+        if k == planes - 2:
+            @pl.when((z > 0) & (z < last))
+            def _():
+                weight_grads()
+
+            both(acts, k)
+            forward_both(k - 1)
         for part in range(GPARTS):
             chain_wait(gg, zg_s, zg_r, k, part)
             if k < planes - 2:
                 chain_start(gg, zg_s, zg_r, k + 1, part)
             both(functools.partial(dispatch_g, part=part), k)
-        both(acts, k)
-        if k > 0:
-            forward_both(k - 1)
+        if k < planes - 2:
+            both(acts, k)
+            if k > 0:
+                forward_both(k - 1)
     both(grads, planes - 2)
-
-    is_end = jnp.where((z == 0) | (z == last), 1, 0)
-
-    @pl.loop(0, 2)
-    def _(phase):
-        @pl.when(phase == is_end)
-        def _():
-            for p in range(planes):
-                for i, (src, dst) in enumerate(((rows, rows_h), (scaled, scaled_h))):
-                    for cp in halves(src, dst, i, p):
-                        cp.wait()
-                for i, ref in enumerate((gate_gr, up_gr, hid)):
-                    rep_copy(ref, 2 + i, p).wait()
-            weight_in(rows_h, gate_gr, gwo_v)
-            out_copy(0).start()
-            weight_in(rows_h, up_gr, uwo_v)
-            out_copy(1).start()
-            weight_down()
-            out_copy(2).start()
-
-        @pl.when(phase == 0)
-        def _():
-            forward_both(planes - 2)
+    forward_both(planes - 2)
+
+    @pl.when((z == 0) | (z == last))
+    def _():
+        weight_grads()
 
     @pl.loop(0, PIECES)
     def _(q):
@@ -431,25 +436,6 @@
         def _(p=p):
             for q in range(PIECES):
                 ret_copy(0, p, q).wait_send()
-
-
-def hand_over(*refs):
-    srcs, dsts, held, sems = refs[:4], refs[4:8], refs[8:12], refs[12]
-    loads, stores = [], []
-    for i in range(4):
-        axis = len(srcs[i].shape) - 2
-        piece = srcs[i].shape[axis] // PIECES
-        for q in range(PIECES):
-            at = (0,) * axis + (pl.ds(q * piece, piece),)
-            loads.append(pltpu.make_async_copy(srcs[i].at[at], held[i].at[at], sems.at[0, i, q]))
-            stores.append(pltpu.make_async_copy(held[i].at[at], dsts[i].at[at], sems.at[1, i, q]))
-    for cp in loads:
-        cp.start()
-    for load, store in zip(loads, stores):
-        load.wait()
-        store.start()
-    for cp in stores:
-        cp.wait()
 
 
 def chained(inputs, out_grad, expert_ids, gates, gate_w, up_w, down_w):
@@ -486,7 +472,7 @@
         dma((planes, COLS - 1, PIECES)), dma((planes, COLS - 1, PIECES)),
         dma((planes, PIECES)), dma((2, planes, PIECES)), dma((5, planes)), dma((5, planes)), dma((2, planes)), dma((3,)),
     ]
-    results = pl.pallas_call(
+    return pl.pallas_call(
         functools.partial(layer_kernel, planes, experts, cap),
         out_shape=(
             jax.ShapeDtypeStruct((tok, feat), BF16),
@@ -498,20 +484,12 @@
         out_specs=(vmem, hbm, hbm, hbm),
         scratch_shapes=scratch,
         compiler_params=pltpu.CompilerParams(
-            collective_id=0, has_side_effects=True, vmem_limit_bytes=60 * 1024 * 1024
+            collective_id=0, has_side_effects=True, vmem_limit_bytes=50 * 1024 * 1024
         ),
         cost_estimate=pl.CostEstimate(
             flops=18 * total * feat * hidden_n, bytes_accessed=8 * feat * hidden_n, transcendentals=total * hidden_n
         ),
     )(expert_ids.T, gates.T, inputs, out_grad, gate_w, up_w, down_w)
-    return pl.pallas_call(
-        hand_over,
-        out_shape=tuple(jax.ShapeDtypeStruct(a.shape, a.dtype) for a in results),
-        in_specs=[hbm] * 4,
-        out_specs=(hbm,) * 4,
-        scratch_shapes=[pltpu.VMEM(a.shape, a.dtype) for a in results] + [dma((2, 4, PIECES))],
-        compiler_params=pltpu.CompilerParams(vmem_limit_bytes=16 * 1024 * 1024),
-    )(*results)
 
 
 def arrange(received, owners, local_exp, capacity):

time: 129 us -> 126 us (0.977)
  Pallas kernels: 122 us -> 116 us
  local copies, waits for them, and re-layouts: 5.26 us -> 9.32 us
    pallas_call x1 -> x0, Pallas kernels: 5.49 us -> none  [chained(): pl.pallas_call(hand_over, out_shape=tuple((jax.ShapeDtypeStruct(a.shape,...]
    unnamed x8 -> x16, local copies, waits for them, and re-layouts: 5.26 us -> 9.32 us
where the time goes in v5:
time: 126 us; the launch traced here: 125 us
  Pallas kernels  116 us (92%)
  local copies, waits for them, and re-layouts  9.32 us (7%)
    pallas_call x1, Pallas kernels, chained(): pl.pallas_call(functools.partial(layer_kernel, planes, experts, cap), out...  116 us
    unnamed x16, local copies, waits for them, and re-layouts  9.32 us

profile of v5, /device:TPU:0, one launch (start us, length us, event | category | flops | bytes accessed | tf_op | source)
XLA Modules:
  0.0 125.5 jit_solution(13464666626029453011)
XLA Ops:
  0.6 0.0 copy-start
  0.6 1.0 copy-done
  1.7 0.0 copy-start.1
  1.7 1.0 copy-done.1
  2.7 0.0 copy-start.2
  2.7 0.7 copy-done.2
  3.4 0.0 copy-start.3
  3.4 0.7 copy-done.3
  4.1 115.5 %shard_map.102 = (bf16[128,2048]{1,0:T(8,128)(2,1)S(1)}, bf16[1,1024,768]{2,1,0:T(8,128)(2,1)S(1)}, bf16[1,1024,768]{2,1,0:T(8,128)(2,1)}, bf16[1,768,1024]{2,1,0:T(8,128)(2,1)}) custom-call(s32[2,128]{1,0:T(2,128)S(1)} %bitcast.2, f32[2,128]{1,0:T(2,128)S(1)} %bitcast.3, bf16[128,2048]{1,0:T(8,128)(2,1)S(1)} %copy-done, bf16[128,2048]{1,0:T(8,128)(2,1)S(1)} %copy-done.1, ...), custom_call_target="tpu_custom_call" | custom-call | flops 14495514624 | bytes 12582912 | tf_op jit(solution)/shard_map/pallas_call | solution.py:475
  119.6 0.8 copy.15
  120.4 0.0 copy-start.5
  120.4 1.1 copy.16
  121.5 0.8 copy-done.5
  122.4 0.0 copy-start.4
  122.4 1.1 copy.17
  123.5 0.8 copy-done.4
  124.3 1.1 copy.18
Async XLA Ops:
  0.6 1.0 copy-start
  1.7 1.0 copy-start.1
  2.7 0.7 copy-start.2
  3.4 0.7 copy-start.3
  120.4 2.0 %copy-start.5 = (bf16[1,1024,768]{2,1,0:T(8,128)(2,1)S(1)}, bf16[1,1024,768]{2,1,0:T(8,128)(2,1)}, u32[]{:S(2)}) copy-start(bf16[1,1024,768]{2,1,0:T(8,128)(2,1)} %get-tuple-element.10) | copy-start | bytes 4718596
  122.4 2.0 %copy-start.4 = (bf16[1,768,1024]{2,1,0:T(8,128)(2,1)S(1)}, bf16[1,768,1024]{2,1,0:T(8,128)(2,1)}, u32[]{:S(2)}) copy-start(bf16[1,768,1024]{2,1,0:T(8,128)(2,1)} %get-tuple-element.11) | copy-start | bytes 4718596

commit v6 on v5

--- a/solution.py
+++ b/solution.py
@@ -185,6 +185,9 @@
         st_g[at] = (picked * gate).astype(BF16)
         plane_send(st_g, scaled, pg_s, pg_r, p, part, GPARTS)
 
+    inner = (z > 0) & (z < last)
+    at_end = (z == 0) | (z == last)
+
     def both(fn, k):
         @pl.when(z - 1 - k >= 0)
         def _():
@@ -193,6 +196,13 @@
         @pl.when(z + 1 + k <= last)
         def _():
             fn(jnp.minimum(z + 1 + k, last))
+
+    def work(fn, k):
+        if k < planes - 2:
+            both(fn, k)
+        else:
+            below, above = z - 1 - k, z + 1 + k
+            fn(jnp.where(below >= 0, below, jnp.where(above <= last, above, z)))
 
     def w_copy(i):
         s, d = w_at[i]
@@ -366,7 +376,11 @@
         cp.wait()
     for i in range(3):
         w_copy(i).wait()
-    acts(z)
+
+    @pl.when(at_end)
+    def _():
+        acts(z)
+
     for k in range(planes - 1):
         chain_wait(meta, zm_s, zm_r, k)
         chain_wait(xg, zx_s, zx_r, k)
@@ -375,16 +389,18 @@
             chain_start(xg, zx_s, zx_r, k + 1)
         both(dispatch_x, k)
         if k == 0:
-            grads(z)
+            @pl.when(at_end)
+            def _():
+                grads(z)
         else:
             both(grads, k - 1)
         if k == planes - 2:
-            @pl.when((z > 0) & (z < last))
+            work(acts, k)
+
+            @pl.when(at_end)
             def _():
-                weight_grads()
-
-            both(acts, k)
-            forward_both(k - 1)
+                forward_both(k - 1)
+
         for part in range(GPARTS):
             chain_wait(gg, zg_s, zg_r, k, part)
             if k < planes - 2:
@@ -394,10 +410,16 @@
             both(acts, k)
             if k > 0:
                 forward_both(k - 1)
-    both(grads, planes - 2)
+    work(grads, planes - 2)
+
+    @pl.when(inner)
+    def _():
+        weight_grads()
+        forward_both(planes - 3)
+
     forward_both(planes - 2)
 
-    @pl.when((z == 0) | (z == last))
+    @pl.when(at_end)
     def _():
         weight_grads()
 
@@ -484,7 +506,7 @@
         out_specs=(vmem, hbm, hbm, hbm),
         scratch_shapes=scratch,
         compiler_params=pltpu.CompilerParams(
-            collective_id=0, has_side_effects=True, vmem_limit_bytes=50 * 1024 * 1024
+            collective_id=0, has_side_effects=True, vmem_limit_bytes=56 * 1024 * 1024
         ),
         cost_estimate=pl.CostEstimate(
             flops=18 * total * feat * hidden_n, bytes_accessed=8 * feat * hidden_n, transcendentals=total * hidden_n

time: 126 us -> 126 us (level)
  local copies, waits for them, and re-layouts: 9.32 us -> 7.77 us
    pallas_call x1, Pallas kernels: 116 us -> 117 us  [chained(): pl.pallas_call(functools.partial(layer_kernel, planes, experts, cap), out...]
    unnamed x16 -> x8, local copies, waits for them, and re-layouts: 9.32 us -> 7.77 us
where the time goes in v6:
time: 126 us
  Pallas kernels  117 us (93%)
  local copies, waits for them, and re-layouts  7.77 us (6%)
    pallas_call x1, Pallas kernels, chained(): pl.pallas_call(functools.partial(layer_kernel, planes, experts, cap), out...  117 us
    unnamed x8, local copies, waits for them, and re-layouts  7.77 us

profile of v6, /device:TPU:0, one launch (start us, length us, event | category | flops | bytes accessed | tf_op | source)
XLA Modules:
  0.0 125.8 jit_solution(7500480967318030827)
XLA Ops:
  0.6 117.4 %shard_map.102 = (bf16[128,2048]{1,0:T(8,128)(2,1)}, bf16[1,1024,768]{2,1,0:T(8,128)(2,1)}, bf16[1,1024,768]{2,1,0:T(8,128)(2,1)}, bf16[1,768,1024]{2,1,0:T(8,128)(2,1)}) custom-call(s32[2,128]{1,0:T(2,128)} %bitcast.2, f32[2,128]{1,0:T(2,128)} %bitcast.3, bf16[128,2048]{1,0:T(8,128)(2,1)} %x_hbm.1, bf16[128,2048]{1,0:T(8,128)(2,1)} %g_hbm.1, ...), custom_call_target="tpu_custom_call" | custom-call | flops 14495514624 | bytes 12582912 | tf_op jit(solution)/shard_map/pallas_call | solution.py:497
  118.0 1.9 %copy.15 = bf16[128,2048]{1,0:T(8,128)(2,1)} copy(bf16[128,2048]{1,0:T(8,128)(2,1)} %get-tuple-element.8) | data formatting | bytes 1048576
  119.9 0.0 copy-start.1
  119.9 2.8 %copy.16 = bf16[1,1024,768]{2,1,0:T(8,128)(2,1)} copy(bf16[1,1024,768]{2,1,0:T(8,128)(2,1)} %get-tuple-element.9) | data formatting | bytes 3145728
  122.7 0.0 copy-done.1
  122.7 0.0 copy-start
  122.7 1.1 copy.17
  123.8 0.8 copy-done
  124.7 1.1 copy.18
Async XLA Ops:
  119.9 2.8 %copy-start.1 = (bf16[1,1024,768]{2,1,0:T(8,128)(2,1)S(1)}, bf16[1,1024,768]{2,1,0:T(8,128)(2,1)}, u32[]{:S(2)}) copy-start(bf16[1,1024,768]{2,1,0:T(8,128)(2,1)} %get-tuple-element.10) | copy-start | bytes 4718596
  122.7 2.0 %copy-start = (bf16[1,768,1024]{2,1,0:T(8,128)(2,1)S(1)}, bf16[1,768,1024]{2,1,0:T(8,128)(2,1)}, u32[]{:S(2)}) copy-start(bf16[1,768,1024]{2,1,0:T(8,128)(2,1)} %get-tuple-element.11) | copy-start | bytes 4718596

commit v7 on v6

--- a/solution.py
+++ b/solution.py
@@ -506,7 +506,7 @@
         out_specs=(vmem, hbm, hbm, hbm),
         scratch_shapes=scratch,
         compiler_params=pltpu.CompilerParams(
-            collective_id=0, has_side_effects=True, vmem_limit_bytes=56 * 1024 * 1024
+            collective_id=0, has_side_effects=True, vmem_limit_bytes=50 * 1024 * 1024
         ),
         cost_estimate=pl.CostEstimate(
             flops=18 * total * feat * hidden_n, bytes_accessed=8 * feat * hidden_n, transcendentals=total * hidden_n

time: 126 us -> 126 us (level)
  local copies, waits for them, and re-layouts: 7.77 us -> 9.32 us
    pallas_call x1, Pallas kernels: 117 us -> 116 us  [chained(): pl.pallas_call(functools.partial(layer_kernel, planes, experts, cap), out...]
    unnamed x8 -> x16, local copies, waits for them, and re-layouts: 7.77 us -> 9.32 us
where the time goes in v7:
time: 126 us
  Pallas kernels  116 us (92%)
  local copies, waits for them, and re-layouts  9.32 us (7%)
    pallas_call x1, Pallas kernels, chained(): pl.pallas_call(functools.partial(layer_kernel, planes, experts, cap), out...  116 us
    unnamed x16, local copies, waits for them, and re-layouts  9.32 us

profile of v7, /device:TPU:0, one launch (start us, length us, event | category | flops | bytes accessed | tf_op | source)
XLA Modules:
  0.0 125.8 jit_solution(9330964611712064560)
XLA Ops:
  0.6 0.0 copy-start
  0.6 1.0 copy-done
  1.7 0.0 copy-start.1
  1.7 1.0 copy-done.1
  2.7 0.0 copy-start.2
  2.7 0.7 copy-done.2
  3.4 0.0 copy-start.3
  3.4 0.7 copy-done.3
  4.1 115.8 %shard_map.102 = (bf16[128,2048]{1,0:T(8,128)(2,1)S(1)}, bf16[1,1024,768]{2,1,0:T(8,128)(2,1)S(1)}, bf16[1,1024,768]{2,1,0:T(8,128)(2,1)}, bf16[1,768,1024]{2,1,0:T(8,128)(2,1)}) custom-call(s32[2,128]{1,0:T(2,128)S(1)} %bitcast.2, f32[2,128]{1,0:T(2,128)S(1)} %bitcast.3, bf16[128,2048]{1,0:T(8,128)(2,1)S(1)} %copy-done, bf16[128,2048]{1,0:T(8,128)(2,1)S(1)} %copy-done.1, ...), custom_call_target="tpu_custom_call" | custom-call | flops 14495514624 | bytes 12582912 | tf_op jit(solution)/shard_map/pallas_call | solution.py:497
  119.9 0.8 copy.15
  120.7 0.0 copy-start.5
  120.7 1.1 copy.16
  121.9 0.8 copy-done.5
  122.7 0.0 copy-start.4
  122.7 1.1 copy.17
  123.8 0.8 copy-done.4
  124.7 1.1 copy.18
Async XLA Ops:
  0.6 1.0 copy-start
  1.7 1.0 copy-start.1
  2.7 0.7 copy-start.2
  3.4 0.7 copy-start.3
  120.7 2.0 %copy-start.5 = (bf16[1,1024,768]{2,1,0:T(8,128)(2,1)S(1)}, bf16[1,1024,768]{2,1,0:T(8,128)(2,1)}, u32[]{:S(2)}) copy-start(bf16[1,1024,768]{2,1,0:T(8,128)(2,1)} %get-tuple-element.10) | copy-start | bytes 4718596
  122.7 2.0 %copy-start.4 = (bf16[1,768,1024]{2,1,0:T(8,128)(2,1)S(1)}, bf16[1,768,1024]{2,1,0:T(8,128)(2,1)}, u32[]{:S(2)}) copy-start(bf16[1,768,1024]{2,1,0:T(8,128)(2,1)} %get-tuple-element.11) | copy-start | bytes 4718596
